TPU v7x, 128 devices: a whole 4x4x4 slice. The times are simulated.
128 devices in a mesh: group: 4 (over x_hi, core), tensor: 32 (over x_lo, y, z).
Axes of the slice: x: 4 (x_hi: 2, x_lo: 2; x = x_hi * 2 + x_lo), y: 4, z: 4, core: 2. Of those that a mesh axis runs over, the one named last changes fastest.
Arguments:
- tokens: bfloat16 [4096, 4096], P(('group', 'tensor')), may hold values from -6 to 6
- expert_norm_gain: float32 [4096], replicated, may hold values from 0.1 to 1.9
- routing: int32 [4096, 4], P('group'), may hold values from 0 to 15, all different within a row; in each aligned block of 32 rows (0 to 31, 32 to 63, ...) at most 16 rows name the same one
- chosen_expert_weights: float32 [4096, 4], P('group'), may hold values from 0.05 to 1
- resident_gate_weight: bfloat16 [4096, 24576], P(None, 'tensor'), may hold values from -0.09375 to 0.09375
- resident_up_weight: bfloat16 [4096, 24576], P(None, 'tensor'), may hold values from -0.09375 to 0.09375
- resident_down_weight: bfloat16 [24576, 4096], P('tensor'), may hold values from -0.15625 to 0.15625
- adapter_input_left: bfloat16 [2, 4096, 1024], P(None, 'group', 'tensor'), may hold values from -0.09375 to 0.09375
- adapter_input_right: bfloat16 [2, 64, 24576], P(None, 'group', 'tensor'), may hold values from -0.75 to 0.75
- adapter_output_left: bfloat16 [24576, 64], P('tensor', 'group'), may hold values from -0.15625 to 0.15625
- adapter_output_right: bfloat16 [64, 65536], P('group', 'tensor'), may hold values from -0.75 to 0.75
Outputs:
- mixed: bfloat16 [4096, 4096], P(('group', 'tensor'))
Inputs may be any that keep to these rules, and one draw needn't show every extreme that they name: `routing`: each row names 4 different experts. Within each aligned block of 32 rows (the rows of one device) no expert is named by more than 16 rows, a bound that some block reaches.
All inputs are finite; a program needn't handle non-finite values.
Results may differ from a plain program's by a relative error of at most 0.017.
Values may be sent and summed in bfloat16 or wider, within the bound.
No kernel may reach another device: no remote copies, remote signals or barrier semaphores. Data moves between devices by JAX's collectives and lax.ppermute only.
A program may use at most 128 MiB of HBM per device.

v0:
```python
import jax
import jax.numpy as jnp
from jax import lax
from jax.sharding import PartitionSpec as P

adapter_scale = 0.5
norm_eps = 1e-06


def from_partner(value, axis, bit):
    return lax.ppermute(value, axis, [(i, i ^ 1 << bit) for i in range(lax.axis_size(axis))])


def normalize(rows_in, expert_norm_gain):
    widened = rows_in.astype(jnp.float32)
    spread = jnp.mean(widened * widened, axis=-1, keepdims=True)
    return (widened * lax.rsqrt(spread + norm_eps) * expert_norm_gain).astype(jnp.bfloat16)


def merge_factor_pair(base_matrix, left, right):
    delta_matrix = jnp.dot(left, right, preferred_element_type=jnp.float32)
    return (base_matrix.astype(jnp.float32) + adapter_scale * delta_matrix).astype(jnp.bfloat16)


def slot_table(route_rows, weight_rows, expert_number, capacity):
    chosen = route_rows == expert_number
    routed = jnp.any(chosen, axis=1)
    weight = jnp.sum(jnp.where(chosen, weight_rows, jnp.zeros_like(weight_rows)), axis=1)
    slot_place = jnp.cumsum(routed.astype(jnp.int32)) - 1
    target = jnp.where(routed, slot_place, capacity)
    row_ids = jnp.arange(route_rows.shape[0], dtype=jnp.int32)
    row_index = jnp.zeros((capacity,), jnp.int32).at[target].set(row_ids, mode="drop")
    slot_weight = jnp.zeros((capacity,), weight_rows.dtype).at[target].set(weight, mode="drop")
    return (row_index, slot_weight)


def slot_outputs(picked, slot_weight, merged_gate, merged_up, combined_down_weight):
    gate_value = jnp.dot(picked, merged_gate, preferred_element_type=jnp.float32)
    upward = jnp.dot(picked, merged_up, preferred_element_type=jnp.float32)
    hidden = (jax.nn.silu(gate_value) * upward).astype(jnp.bfloat16)
    output = (
        jnp.dot(hidden, combined_down_weight, preferred_element_type=jnp.float32)
        * slot_weight[:, None]
    )
    return output.astype(jnp.bfloat16)


def expert_term(normed, row_index, slot_weight, merged_gate, merged_up, combined_down_weight):
    picked = normed[row_index]
    output = slot_outputs(picked, slot_weight, merged_gate, merged_up, combined_down_weight).astype(
        jnp.float32
    )
    empty = jnp.zeros((normed.shape[0], normed.shape[1]), jnp.float32)
    return empty.at[row_index].add(output)


def on_device(
    tokens,
    expert_norm_gain,
    routing,
    chosen_expert_weights,
    resident_gate_weight,
    resident_up_weight,
    resident_down_weight,
    adapter_input_left,
    adapter_input_right,
    adapter_output_left,
    adapter_output_right,
):
    position = lax.axis_index("tensor")
    expert_number = position // 2
    lower_half = position % 2 == 0

    def pair_join(mine, other, axis_dim):
        return jnp.where(
            lower_half,
            jnp.concatenate((mine, other), axis_dim),
            jnp.concatenate((other, mine), axis_dim),
        )

    input_left_factor, input_right_factor, left_out, right_out = (
        lax.all_gather(adapter_input_left, "group", axis=1, tiled=True),
        lax.all_gather(adapter_input_right, "group", axis=1, tiled=True),
        lax.all_gather(adapter_output_left, "group", axis=1, tiled=True),
        lax.all_gather(adapter_output_right, "group", axis=0, tiled=True),
    )
    received = from_partner(
        jnp.concatenate((input_left_factor.reshape(-1), right_out.reshape(-1))), "tensor", 0
    )
    count_first = input_left_factor.size
    other_left = received[:count_first].reshape(input_left_factor.shape)
    other_right = received[count_first:].reshape(right_out.shape)
    input_left_factor = pair_join(input_left_factor, other_left, 2)
    right_out = pair_join(right_out, other_right, 1)
    merged_gate = merge_factor_pair(
        resident_gate_weight, input_left_factor[0], input_right_factor[0]
    )
    merged_up = merge_factor_pair(resident_up_weight, input_left_factor[1], input_right_factor[1])
    combined_down_weight = merge_factor_pair(resident_down_weight, left_out, right_out)
    row_total = routing.shape[0]
    top_count = routing.shape[1]
    slice_rows = tokens.shape[0]
    devices_here = lax.axis_size("tensor")
    experts = devices_here // 2
    device_cap = min(slice_rows, max(2, 2 * slice_rows * top_count // experts))
    capacity = min(row_total, devices_here * device_cap)
    whole_rows = lax.all_gather(tokens, "tensor", axis=0, tiled=True)
    normed = normalize(whole_rows, expert_norm_gain)
    row_index, slot_weight = slot_table(routing, chosen_expert_weights, expert_number, capacity)
    partial_value = expert_term(
        normed, row_index, slot_weight, merged_gate, merged_up, combined_down_weight
    )
    summed = lax.psum(partial_value.astype(jnp.bfloat16), "tensor").astype(jnp.float32)
    own_rows = lax.dynamic_slice_in_dim(summed, position * slice_rows, slice_rows, 0)
    return own_rows.astype(jnp.bfloat16)


def solution(mesh):
    return jax.shard_map(
        on_device,
        mesh=mesh,
        in_specs=(
            P(("group", "tensor"), None),
            P(),
            P("group", None),
            P("group", None),
            P(None, "tensor"),
            P(None, "tensor"),
            P("tensor", None),
            P(None, "group", "tensor"),
            P(None, "group", "tensor"),
            P("tensor", "group"),
            P("group", "tensor"),
        ),
        out_specs=P(("group", "tensor"), None),
        check_vma=False,
    )
```

profile of v0, /device:TPU:10, one launch (start us, length us, event | category | flops | bytes accessed | tf_op | source)
XLA Modules:
  0.0 618.0 jit_solution(9001694400215584515)
XLA Ops:
  7.3 7.5 %all_gather.17 = bf16[64,2048]{1,0:T(8,128)(2,1)S(1)} all-gather(bf16[16,2048]{1,0:T(8,128)(2,1)} %param.21), channel_id=1, replica_groups=mesh['group'=4,'tensor'=32] {'group'}, dimensions={0}, use_global_device_ids=true | all-gather | bytes 327680 | tf_op jit(solution)/shard_map/all_gather | solution.py:85
  14.9 1.2 copy.15
  16.0 17.3 %all_gather.16 = bf16[2,4096,32]{2,1,0:T(8,128)(2,1)S(1)} all-gather(bf16[2,1024,32]{2,1,0:T(8,128)(2,1)S(1)} %copy.15), channel_id=1, replica_groups=mesh['group'=4,'tensor'=32] {'group'}, dimensions={1}, use_global_device_ids=true | all-gather | bytes 655360 | tf_op jit(solution)/shard_map/all_gather | solution.py:82
  35.5 1.9 collective-permute-start
  37.8 8.8 %copy.14 = bf16[4096,768]{0,1:T(8,128)(2,1)} copy(bf16[4096,768]{1,0:T(8,128)(2,1)} %param.15) | data formatting | bytes 12582912 | tf_op args[4]
  46.6 8.7 %copy.16 = bf16[4096,768]{0,1:T(8,128)(2,1)} copy(bf16[4096,768]{1,0:T(8,128)(2,1)} %param.16) | data formatting | bytes 12582912 | tf_op args[5]
  55.5 4.3 scatter_custom_fusion
  59.8 4.3 scatter_custom_fusion.1
  64.1 6.8 %all_gather.19 = bf16[768,64]{0,1:T(8,128)(2,1)S(1)} all-gather(bf16[768,16]{0,1:T(8,128)(2,1)S(1)} %copy-done.2), channel_id=1, replica_groups=mesh['group'=4,'tensor'=32] {'group'}, dimensions={1}, use_global_device_ids=true | all-gather | bytes 122880 | tf_op jit(solution)/shard_map/all_gather | solution.py:84
  71.0 7.3 %all_gather.18 = bf16[2,64,768]{2,1,0:T(8,128)(2,1)S(1)} all-gather(bf16[2,16,768]{2,1,0:T(8,128)(2,1)S(1)} %copy-done.1), channel_id=1, replica_groups=mesh['group'=4,'tensor'=32] {'group'}, dimensions={1}, use_global_device_ids=true | all-gather | bytes 245760 | tf_op jit(solution)/shard_map/all_gather | solution.py:83
  79.4 1.1 slice.58
  80.5 1.8 slice.48
  82.3 5.9 maximum_select_fusion
  88.2 89.4 %all-gather.2.cloned.1.call-done = bf16[1024,4096]{1,0:T(8,128)(2,1)} async-done(((bf16[32,4096]{1,0:T(8,128)(2,1)}), bf16[1024,4096]{1,0:T(8,128)(2,1)}) %all-gather.2.cloned.1.call-update) | async-done | bytes 8388624 | tf_op jit(solution)/shard_map/all_gather | solution.py:107
  177.6 5.1 fusion
  182.7 10.3 %fusion.2 = bf16[1024,4096]{1,0:T(8,128)(2,1)} fusion(bf16[1024,4096]{1,0:T(8,128)(2,1)} %all-gather.2.cloned.1.call-done, f32[4096]{0:T(1024)S(1)} %copy-done.5, f32[1024]{0:T(1024)S(1)} %add_rsqrt_fusion), kind=kLoop, calls=%fused_computation.8 | loop fusion | flops 16777216 | bytes 16797696 | tf_op jit(solution)/shard_map/convert_element_type | solution.py:17
  193.1 13.5 %gather_fusion = bf16[512,4096]{1,0:T(8,128)(2,1)} fusion(bf16[1024,4096]{1,0:T(8,128)(2,1)} %fusion.2, s32[1024]{0:T(1024)S(1)} %pad_clamp_fusion), kind=kCustom, calls=%fused_computation | custom fusion | bytes 8390656 | tf_op jit(solution)/shard_map/gather | solution.py:49
  206.6 10.6 %fusion.8 = f32[512,768]{1,0:T(8,128)} fusion(bf16[512,4096]{1,0:T(8,128)(2,1)} %gather_fusion, bf16[4096,768]{0,1:T(8,128)(2,1)} %copy.16, bf16[2,4096,64]{2,1,0:T(8,128)(2,1)S(1)} %copy-done, bf16[2,64,768]{2,1,0:T(8,128)(2,1)S(1)} %all_gather.18), kind=kOutput, calls=%fused_computation.18 | convolution fusion | flops 3636461568 | bytes 13205504 | tf_op jit(solution)/shard_map/dot_general | solution.py:39
  217.2 10.7 %multiply_convert_fusion.1 = bf16[512,768]{1,0:T(8,128)(2,1)} fusion(f32[512,768]{1,0:T(8,128)} %fusion.8, bf16[512,4096]{1,0:T(8,128)(2,1)} %gather_fusion, bf16[4096,768]{0,1:T(8,128)(2,1)} %copy.14, bf16[2,4096,64]{2,1,0:T(8,128)(2,1)S(1)} %copy-done, bf16[2,64,768]{2,1,0:T(8,128)(2,1)S(1)} %all_gather.18), kind=kOutput, calls=%fused_computation.20 | convolution fusion | flops 3638820864 | bytes 13991936 | tf_op jit(solution)/shard_map/dot_general | solution.py:38
  227.9 9.2 %multiply_convert_fusion = bf16[512,4096]{1,0:T(8,128)(2,1)} fusion(bf16[512,768]{1,0:T(8,128)(2,1)} %multiply_convert_fusion.1, f32[512]{0:T(512)S(1)} %scatter_custom_fusion.1, bf16[768,4096]{1,0:T(8,128)(2,1)} %param.17, bf16[768,64]{0,1:T(8,128)(2,1)S(1)} %all_gather.19, bf16[64,2048]{1,0:T(8,128)(2,1)S(1)} %slice.54, ...), kind=kOutput, calls=%fused_computation.15 | convolution fusion | flops 3643015168 | bytes 11896833 | tf_op jit(solution)/shard_map/dot_general | solution.py:42
  237.1 20.2 %scatter_custom_fusion.2 = f32[1024,4096]{1,0:T(8,128)} fusion(s32[512]{0:T(512)S(1)} %compare_select_fusion.1, bf16[512,4096]{1,0:T(8,128)(2,1)} %multiply_convert_fusion, f32[]{:T(128)} %constant.21.clone.1), kind=kCustom, calls=%fused_computation.13 | custom fusion | flops 4194304 | bytes 20971524 | tf_op jit(solution)/shard_map/scatter-add | solution.py:54
  257.3 9.0 %convert_element_type.62 = bf16[1024,4096]{1,0:T(8,128)(2,1)} convert(f32[1024,4096]{1,0:T(8,128)} %scatter_custom_fusion.2) | non-fusion elementwise | flops 4194304 | bytes 25165824 | tf_op jit(solution)/shard_map/convert_element_type | solution.py:113
  266.3 343.0 %all-reduce.2.cloned.1.call-done = bf16[1024,4096]{1,0:T(8,128)(2,1)} async-done(((bf16[1024,4096]{1,0:T(8,128)(2,1)}), bf16[1024,4096]{1,0:T(8,128)(2,1)}) %all-reduce.2.cloned.1.call-update) | async-done | bytes 8388624 | tf_op jit(solution)/shard_map/psum | solution.py:113
  609.3 1.7 convert_convert_fusion
  (35 shorter events, 4.6 us)
Async XLA Ops:
  6.5 30.9 %copy-start.3 = (f32[1024,4]{0,1:T(4,128)S(1)}, f32[1024,4]{0,1:T(4,128)}, u32[]{:S(2)}) copy-start(f32[1024,4]{0,1:T(4,128)} %param.14) | copy-start | bytes 49156
  6.5 30.9 %copy-start.4 = (s32[1024,4]{0,1:T(4,128)S(1)}, s32[1024,4]{0,1:T(4,128)}, u32[]{:S(2)}) copy-start(s32[1024,4]{0,1:T(4,128)} %param.13) | copy-start | bytes 49156
  6.5 171.1 %all-gather.2.cloned.1.call-start = ((), (), s32[]{:S(2)}) async-start(), calls=%async_computation | async-start | bytes 8650752 | tf_op jit(solution)/shard_map/all_gather | solution.py:107
  7.3 602.1 %all-reduce.2.cloned.1.call-start = ((), (), s32[]{:S(2)}) async-start(), calls=%async_computation.1 | async-start | bytes 16777216 | tf_op jit(solution)/shard_map/psum | solution.py:113
  35.5 42.8 %collective-permute-start = (bf16[393216]{0:T(1024)(128)(2,1)}, bf16[393216]{0:T(1024)(128)(2,1)}, u32[]{:S(2)}, u32[]{:S(2)}) collective-permute-start(bf16[393216]{0:T(1024)(128)(2,1)} %pad_maximum_fusion), channel_id=1, source_target_pairs={{0,1},{1,0},{2,3},{3,2},{4,5},{5,4},{6,7},{7,6},{8,9},{9,8},{10,11... | collective-permute-start | bytes 2359304 | tf_op jit(solution)/shard_map/ppermute | solution.py:11
  46.6 17.5 %copy-start.2 = (bf16[768,16]{0,1:T(8,128)(2,1)S(1)}, bf16[768,16]{0,1:T(8,128)(2,1)}, u32[]{:S(2)}) copy-start(bf16[768,16]{0,1:T(8,128)(2,1)} %param.20) | copy-start | bytes 73732
  46.6 24.4 %copy-start.1 = (bf16[2,16,768]{2,1,0:T(8,128)(2,1)S(1)}, bf16[2,16,768]{2,1,0:T(8,128)(2,1)}, u32[]{:S(2)}) copy-start(bf16[2,16,768]{2,1,0:T(8,128)(2,1)} %param.19) | copy-start | bytes 147460
  82.3 100.4 %copy-start.5 = (f32[4096]{0:T(1024)S(1)}, f32[4096]{0:T(1024)}, u32[]{:S(2)}) copy-start(f32[4096]{0:T(1024)} %param.12) | copy-start | bytes 49156
  193.1 13.6 %copy-start = (bf16[2,4096,64]{2,1,0:T(8,128)(2,1)S(1)}, bf16[2,4096,64]{2,1,0:T(8,128)(2,1)}, u32[]{:S(2)}) copy-start(bf16[2,4096,64]{2,1,0:T(8,128)(2,1)} %maximum_select_fusion) | copy-start | bytes 3145732
Sparse Core Ops, SparseCore 0:
  9.0 168.5 all-gather.1
  266.4 342.8 all-reduce.1
where the time goes:
time: 630 us; the launch traced here: 618 us
  waiting for transfers between devices  433 us (69%)
  other arithmetic  53.7 us (9%)
  local copies, waits for them, and re-layouts  46.1 us (7%)
  blocking collectives  39 us (6%)
  matrix products  30.5 us (5%)
  between operations  13.7 us (2%)
    psum x1, waiting for transfers between devices, on_device(): lax.psum(partial_value.astype(jnp.bfloat16), 'tensor').astype(jnp.float32)  343 us
    all_gather x1, waiting for transfers between devices, on_device(): whole_rows = lax.all_gather(tokens, 'tensor', axis=0, tiled=True)  89.4 us
    scatter-add x1, other arithmetic, expert_term(): return empty.at[row_index].add(output)  20.2 us
    unnamed x16, local copies, waits for them, and re-layouts  18.7 us
    all_gather x1, blocking collectives, on_device(): lax.all_gather(adapter_input_left, 'group', axis=1, tiled=True)  17.3 us
    gather x1, local copies, waits for them, and re-layouts, expert_term(): picked = normed[row_index]  13.5 us
  transfers between devices with their start and end apart: 3, of which 2 were waited for; matrix products, arithmetic and copies ran while one was open for 6% of the time, Pallas kernels for 0%

commit v1 on v0

v1 whole, which is shorter than its diff:
```python
import functools

import jax
import jax.numpy as jnp
from jax import lax
from jax.experimental import pallas as pl
from jax.experimental.pallas import tpu as pltpu
from jax.sharding import PartitionSpec as P

ADAPTER_SCALE = 0.5
NORM_EPS = 1e-06
EXPERTS = 16
CAP = 16
F32 = jnp.float32
BF16 = jnp.bfloat16
NT = (((1,), (1,)), ((), ()))
TN = (((0,), (0,)), ((), ()))


def exchange(value, axis, bit):
    return lax.ppermute(value, axis, [(i, i ^ bit) for i in range(lax.axis_size(axis))])


def slots_of(route_t, copies):
    rows = route_t.shape[1]
    experts = lax.broadcasted_iota(jnp.int32, (EXPERTS, rows), 0)
    chosen = jnp.zeros((EXPERTS, rows), jnp.bool_)
    for k in range(route_t.shape[0]):
        chosen = chosen | (route_t[k : k + 1, :] == experts)
    upper = (
        lax.broadcasted_iota(jnp.int32, (rows, rows), 0)
        <= lax.broadcasted_iota(jnp.int32, (rows, rows), 1)
    ).astype(F32)
    place = jnp.dot(chosen.astype(F32), upper, preferred_element_type=F32).astype(jnp.int32) - 1
    place = jnp.where(chosen, place, -1)
    slot = lax.broadcasted_iota(jnp.int32, (EXPERTS, copies * CAP, rows), 1) % CAP
    return place[:, None, :] == slot


def dispatch_body(tokens_ref, gain_ref, route_ref, out_ref, normed_ref, mask_ref):
    step = pl.program_id(0)

    @pl.when(step == 0)
    def _():
        wide = tokens_ref[...].astype(F32)
        spread = jnp.mean(wide * wide, axis=-1, keepdims=True)
        normed_ref[...] = (wide * lax.rsqrt(spread + NORM_EPS) * gain_ref[...]).astype(BF16)
        mask = slots_of(route_ref[...], 1)
        mask_ref[...] = mask.astype(F32).reshape(EXPERTS * CAP, -1).astype(BF16)

    per = out_ref.shape[0]
    pick = mask_ref[pl.ds(pl.multiple_of(step * per * CAP, per * CAP), per * CAP), :]
    rows = jnp.dot(pick, normed_ref[...], preferred_element_type=F32).astype(BF16)
    for i in range(per):
        out_ref[i, 0] = rows[i * CAP : (i + 1) * CAP]
        out_ref[i, 1] = rows[i * CAP : (i + 1) * CAP]


def dispatch(tokens, gain, route_t):
    rows, width = tokens.shape
    steps = 4
    per = EXPERTS // steps
    return pl.pallas_call(
        dispatch_body,
        grid=(steps,),
        out_shape=jax.ShapeDtypeStruct((EXPERTS, 2, CAP, width), BF16),
        in_specs=[
            pl.BlockSpec((rows, width), lambda i: (0, 0)),
            pl.BlockSpec((1, width), lambda i: (0, 0)),
            pl.BlockSpec(route_t.shape, lambda i: (0, 0)),
        ],
        out_specs=pl.BlockSpec((per, 2, CAP, width), lambda i: (i, 0, 0, 0)),
        scratch_shapes=[pltpu.VMEM((rows, width), BF16), pltpu.VMEM((EXPERTS * CAP, rows), BF16)],
        compiler_params=pltpu.CompilerParams(vmem_limit_bytes=24 << 20),
        cost_estimate=pl.CostEstimate(
            flops=2 * EXPERTS * CAP * rows * width, bytes_accessed=5 << 20, transcendentals=0
        ),
        name="dispatch",
    )(tokens, gain, route_t)


def ffn_body(
    hid_steps, place_ref, x_ref, wg_ref, wu_ref, wd_ref, own_ref, far_ref, out_ref,
    low_ref, right_ref, hidden_ref, mid_ref, outr_ref,
):
    step = pl.program_id(0)
    group, half = place_ref[0], place_ref[1]
    width = hidden_ref.shape[1]
    block = wg_ref.shape[1]
    packs = (own_ref, far_ref)

    @pl.when(step == 0)
    def _():
        right_ref[...] = jnp.zeros_like(right_ref)
        low = None
        for core in range(2):
            for xh in range(2):
                pack = packs[core]
                there = group ^ (xh * 2 + core)
                near, across = xh * 64, 128 + xh * 48
                span = x_ref.shape[1] // 4
                x = x_ref[:, pl.ds(pl.multiple_of(there * span, span), span)]
                left = jnp.concatenate(
                    [
                        pack[near : near + 32, 0:span],
                        pack[near : near + 32, span : 2 * span],
                        pack[across : across + 32, 0:span],
                        pack[across : across + 32, span : 2 * span],
                    ],
                    axis=0,
                )
                term = lax.dot_general(x, left, NT, preferred_element_type=F32)
                low = term if low is None else low + term
                ranks = (half ^ (there >> 1)) * 64 + (there & 1) * 16
                r0 = pl.multiple_of(ranks, 16)
                r1 = pl.multiple_of(ranks + 32, 16)
                right_ref[pl.ds(r0, 16), 0:width] = pack[near + 48 : near + 64, 0:width]
                right_ref[pl.ds(r1, 16), width : 2 * width] = pack[
                    near + 48 : near + 64, width : 2 * width
                ]
                row = (core * 2 + xh) * 16
                cols = outr_ref.shape[2]
                outr_ref[0, row : row + 16, :] = pack[near + 32 : near + 48, 0:cols]
                outr_ref[1, row : row + 16, :] = pack[across + 32 : across + 48, 0:cols]
        low_ref[...] = (ADAPTER_SCALE * low).astype(BF16)

    for n in range(hid_steps):

        @pl.when(step == n)
        def _(n=n):
            x = x_ref[...]
            low = low_ref[...]
            gate = jnp.dot(x, wg_ref[...], preferred_element_type=F32)
            gate += jnp.dot(
                low, right_ref[:, n * block : (n + 1) * block], preferred_element_type=F32
            )
            up = jnp.dot(x, wu_ref[...], preferred_element_type=F32)
            up += jnp.dot(
                low,
                right_ref[:, width + n * block : width + (n + 1) * block],
                preferred_element_type=F32,
            )
            hidden_ref[:, n * block : (n + 1) * block] = (jax.nn.silu(gate) * up).astype(BF16)

    @pl.when(step == hid_steps)
    def _():
        left = jnp.concatenate(
            [
                packs[core][xh * 64 + 48 : xh * 64 + 64, 2 * width : 3 * width]
                for core in range(2)
                for xh in range(2)
            ],
            axis=0,
        )
        mid = lax.dot_general(hidden_ref[...], left, NT, preferred_element_type=F32)
        mid_ref[...] = (ADAPTER_SCALE * mid).astype(BF16)

    @pl.when(step >= hid_steps)
    def _():
        cols = out_ref.shape[1]
        start = (step - hid_steps) * cols
        side = start // outr_ref.shape[2]
        offset = pl.multiple_of(start - side * outr_ref.shape[2], cols)
        out = jnp.dot(hidden_ref[...], wd_ref[...], preferred_element_type=F32)
        out += jnp.dot(
            mid_ref[...], outr_ref[half ^ side, :, pl.ds(offset, cols)], preferred_element_type=F32
        )
        out_ref[...] = out.astype(BF16)


def feed_forward(place, x, wg, wu, wd, own, far):
    rows, width = x.shape
    hidden = wg.shape[1]
    block, cols = 256, 1024
    hid_steps, out_steps = hidden // block, width // cols
    first = lambda i: jnp.minimum(i, hid_steps - 1)
    later = lambda i: jnp.maximum(i - hid_steps, 0)
    whole = lambda a: pl.BlockSpec(a.shape, lambda i, s: (0,) * a.ndim)
    return pl.pallas_call(
        functools.partial(ffn_body, hid_steps),
        grid_spec=pltpu.PrefetchScalarGridSpec(
            num_scalar_prefetch=1,
            grid=(hid_steps + out_steps,),
            in_specs=[
                whole(x),
                pl.BlockSpec((width, block), lambda i, s: (0, first(i))),
                pl.BlockSpec((width, block), lambda i, s: (0, first(i))),
                pl.BlockSpec((hidden, cols), lambda i, s: (0, later(i))),
                whole(own),
                whole(far),
            ],
            out_specs=pl.BlockSpec((rows, cols), lambda i, s: (0, later(i))),
            scratch_shapes=[
                pltpu.VMEM((rows, 128), BF16),
                pltpu.VMEM((128, 2 * hidden), BF16),
                pltpu.VMEM((rows, hidden), BF16),
                pltpu.VMEM((rows, 64), BF16),
                pltpu.VMEM((2, 64, width // 2), BF16),
            ],
        ),
        out_shape=jax.ShapeDtypeStruct((rows, width), BF16),
        compiler_params=pltpu.CompilerParams(vmem_limit_bytes=48 << 20),
        cost_estimate=pl.CostEstimate(
            flops=6 * rows * width * hidden, bytes_accessed=28 << 20, transcendentals=rows * hidden
        ),
        name="feed_forward",
    )(place, x, wg, wu, wd, own, far)


def combine_body(route_ref, weight_ref, part_ref, out_ref, high_ref, low_ref):
    @pl.when(pl.program_id(0) == 0)
    def _():
        route_t, weight_t = route_ref[...], weight_ref[...]
        rows = route_t.shape[1]
        experts = lax.broadcasted_iota(jnp.int32, (EXPERTS, rows), 0)
        weight = jnp.zeros((EXPERTS, rows), F32)
        for k in range(route_t.shape[0]):
            weight += jnp.where(route_t[k : k + 1, :] == experts, weight_t[k : k + 1, :], 0.0)
        mask = slots_of(route_t, 2)
        spread = jnp.where(mask, weight[:, None, :], 0.0).reshape(2 * EXPERTS * CAP, rows)
        high = spread.astype(BF16)
        high_ref[...] = high
        low_ref[...] = (spread - high.astype(F32)).astype(BF16)

    part = part_ref[...]
    total = lax.dot_general(high_ref[...], part, TN, preferred_element_type=F32)
    total += lax.dot_general(low_ref[...], part, TN, preferred_element_type=F32)
    out_ref[...] = total.astype(BF16)


def combine(route_t, weight_t, part):
    slots, width = part.shape
    rows = route_t.shape[1]
    cols = 1024
    return pl.pallas_call(
        combine_body,
        grid=(width // cols,),
        out_shape=jax.ShapeDtypeStruct((rows, width), BF16),
        in_specs=[
            pl.BlockSpec(route_t.shape, lambda i: (0, 0)),
            pl.BlockSpec(weight_t.shape, lambda i: (0, 0)),
            pl.BlockSpec((slots, cols), lambda i: (0, i)),
        ],
        out_specs=pl.BlockSpec((rows, cols), lambda i: (0, i)),
        scratch_shapes=[pltpu.VMEM((slots, rows), BF16), pltpu.VMEM((slots, rows), BF16)],
        compiler_params=pltpu.CompilerParams(vmem_limit_bytes=24 << 20),
        cost_estimate=pl.CostEstimate(
            flops=4 * slots * rows * width, bytes_accessed=5 << 20, transcendentals=0
        ),
        name="combine",
    )(route_t, weight_t, part)


def gather_factors(input_left, input_right, output_left, output_right):
    left = jnp.transpose(input_left, (2, 0, 1)).reshape(input_left.shape[2], -1)
    right = jnp.concatenate([input_right[0], input_right[1], output_left.T], axis=1)
    wide = right.shape[1]
    pad = lambda a: jnp.pad(a, ((0, 0), (0, wide - a.shape[1])))
    mine = jnp.concatenate([pad(left), pad(output_right), right], axis=0)
    shared = left.shape[0] + output_right.shape[0]
    across_x = exchange(mine, "group", 2)
    partner = exchange(jnp.concatenate([mine[:shared], across_x[:shared]], axis=0), "tensor", 1)
    own = jnp.concatenate([mine, across_x, partner], axis=0)
    return own, exchange(own, "group", 1)


def on_device(
    tokens,
    expert_norm_gain,
    routing,
    chosen_expert_weights,
    resident_gate_weight,
    resident_up_weight,
    resident_down_weight,
    adapter_input_left,
    adapter_input_right,
    adapter_output_left,
    adapter_output_right,
):
    rows, width = tokens.shape
    position = lax.axis_index("tensor")
    place = jnp.stack([lax.axis_index("group"), position % 2]).astype(jnp.int32)
    own, far = gather_factors(
        adapter_input_left, adapter_input_right, adapter_output_left, adapter_output_right
    )
    route_t = lax.dynamic_slice_in_dim(routing, position * rows, rows, 0).T
    weight_t = lax.dynamic_slice_in_dim(chosen_expert_weights, position * rows, rows, 0).T
    sent = dispatch(tokens, expert_norm_gain.reshape(1, width), route_t)
    sent = sent.reshape(2 * EXPERTS, CAP, width)
    x = lax.all_to_all(sent, "tensor", 0, 0, tiled=True).reshape(2 * EXPERTS * CAP, width)
    part = feed_forward(
        place, x, resident_gate_weight, resident_up_weight, resident_down_weight, own, far
    )
    part = part.reshape(2 * EXPERTS, CAP, width)
    back = lax.all_to_all(part, "tensor", 0, 0, tiled=True).reshape(2 * EXPERTS * CAP, width)
    return combine(route_t, weight_t, back)


def solution(mesh):
    return jax.shard_map(
        on_device,
        mesh=mesh,
        in_specs=(
            P(("group", "tensor"), None),
            P(),
            P("group", None),
            P("group", None),
            P(None, "tensor"),
            P(None, "tensor"),
            P("tensor", None),
            P(None, "group", "tensor"),
            P(None, "group", "tensor"),
            P("tensor", "group"),
            P("group", "tensor"),
        ),
        out_specs=P(("group", "tensor"), None),
        check_vma=False,
    )
```

time: 630 us -> 178 us (0.28); the launches traced: 618 us -> 177 us
  waiting for transfers between devices: 433 us -> 124 us
  other arithmetic: 53.7 us -> 0.14 us
  local copies, waits for them, and re-layouts: 46.1 us -> 5.31 us
  blocking collectives: 39 us -> 0 us
  matrix products: 30.5 us -> 0 us
  Pallas kernels: 0 us -> 27.9 us
  starting transfers between devices: 1.97 us -> 19.8 us
  between operations: 13.7 us -> 0.15 us
    psum x1 -> x0, waiting for transfers between devices: 343 us -> none  [on_device(): lax.psum(partial_value.astype(jnp.bfloat16), 'tensor').astype(jnp.float32)]
    all_gather x1 -> x0, waiting for transfers between devices: 89.4 us -> none  [on_device(): whole_rows = lax.all_gather(tokens, 'tensor', axis=0, tiled=True)]
    ppermute x1 -> x3, waiting for transfers between devices: 0.01 us -> 68.7 us  [exchange(): lax.ppermute(value, axis, [(i, i ^ bit) for i in range(lax.axis_size(axis...]
    all_to_all x0 -> x2, waiting for transfers between devices: none -> 55.2 us  [the longest x1 55.2 us: on_device(): lax.all_to_all(part, 'tensor', 0, 0, tiled=True)]
    all_gather x4 -> x0, blocking collectives: 39 us -> none  [the longest x1 17.3 us: on_device(): lax.all_gather(adapter_input_left, 'group', axis=1, tiled=True)]
    dot_general x3 -> x0, matrix products: 30.5 us -> none  [the longest x1 10.7 us: slot_outputs(): jnp.dot(picked, merged_gate, preferred_element_type=jnp.float32)]
    pallas_call x0 -> x3, Pallas kernels: none -> 27.9 us  [the longest x1 21.5 us: feed_forward(): pl.pallas_call(functools.partial(ffn_body, hid_steps), grid_spec=pltpu.Pr...]
    convert_element_type x4 -> x0, other arithmetic: 21 us -> none  [the longest x1 10.3 us: normalize(): (widened * lax.rsqrt(spread + norm_eps) * expert_norm_gain).astype(jnp.bf...]
  transfers between devices with their start and end apart: 3 -> 5, of which waited for: 2 -> 4; matrix products, arithmetic and copies ran while one was open for 6% -> 1% of each run, Pallas kernels for 0% -> 0%
where the time goes in v1:
time: 178 us; the launch traced here: 177 us
  waiting for transfers between devices  124 us (70%)
  Pallas kernels  27.9 us (16%)
  starting transfers between devices  19.8 us (11%)
  local copies, waits for them, and re-layouts  5.31 us (3%)
    ppermute x3, waiting for transfers between devices, exchange(): lax.ppermute(value, axis, [(i, i ^ bit) for i in range(lax.axis_size(axis...  68.7 us
    all_to_all x1, waiting for transfers between devices, on_device(): lax.all_to_all(part, 'tensor', 0, 0, tiled=True)  55.2 us
    pallas_call x1, Pallas kernels, feed_forward(): pl.pallas_call(functools.partial(ffn_body, hid_steps), grid_spec=pltpu.Pr...  21.5 us
    all_to_all x1, starting transfers between devices, on_device(): lax.all_to_all(sent, 'tensor', 0, 0, tiled=True)  9.66 us
    all_to_all x1, starting transfers between devices, on_device(): lax.all_to_all(part, 'tensor', 0, 0, tiled=True)  7.38 us
    pallas_call x1, Pallas kernels, combine(): pl.pallas_call(combine_body, grid=(width // cols,), out_shape=jax.ShapeDt...  4.98 us
    unnamed x17, local copies, waits for them, and re-layouts  4.39 us
  transfers between devices with their start and end apart: 5, of which 4 were waited for; matrix products, arithmetic and copies ran while one was open for 1% of the time, Pallas kernels for 0%

profile of v1, /device:TPU:10, one launch (start us, length us, event | category | flops | bytes accessed | tf_op | source)
XLA Modules:
  0.0 177.1 jit_solution(7480586301311140755)
XLA Ops:
  0.0 0.0 copy-start
  0.0 0.7 copy-done
  0.7 0.1 dynamic-slice_bitcast_fusion.1.route_ref
  0.8 0.9 copy-done.2
  1.7 0.7 copy-done.3
  2.5 1.4 dispatch.1
  3.8 0.0 copy-start.1
  3.9 2.0 %copy-done.1 = bf16[16,2,16,4096]{3,2,1,0:T(8,128)(2,1)} copy-done((bf16[16,2,16,4096]{3,2,1,0:T(8,128)(2,1)}, bf16[16,2,16,4096]{3,2,1,0:T(8,128)(2,1)S(1)}, u32[]{:S(2)}) %copy-start.1) | copy-done | bytes 4194328
  5.8 9.7 %all-to-all-start = ((bf16[32,16,4096]{2,1,0:T(8,128)(2,1)}), bf16[32,16,4096]{2,1,0:T(8,128)(2,1)}, u32[]{:S(2)}, u32[]{:S(2)}) async-start(bf16[32,16,4096]{2,1,0:T(8,128)(2,1)} %bitcast.19), calls=%async_computation | async-start | bytes 8388608 | tf_op jit(solution)/shard_map/all_to_all | solution.py:290
  15.5 0.0 copy-done.4
  15.5 0.0 copy-done.7
  15.6 2.2 %collective-permute-start = (bf16[64,2304]{1,0:T(8,128)(2,1)S(1)}, bf16[64,2304]{1,0:T(8,128)(2,1)S(1)}, u32[]{:S(2)}, u32[]{:S(2)}) collective-permute-start(bf16[64,2304]{1,0:T(8,128)(2,1)S(1)} %maximum_maximum_fusion), channel_id=1, source_target_pairs={{0,64},{32,96},{64,0},{96,32},{1,65},{33,97},{65,1},{97,33},{2,66}... | collective-permute-start | bytes 884744 | tf_op jit(solution)/shard_map/ppermute | solution.py:21
  17.9 55.8 %collective-permute-done = bf16[64,2304]{1,0:T(8,128)(2,1)S(1)} collective-permute-done((bf16[64,2304]{1,0:T(8,128)(2,1)S(1)}, bf16[64,2304]{1,0:T(8,128)(2,1)S(1)}, u32[]{:S(2)}, u32[]{:S(2)}) %collective-permute-start) | collective-permute-done | bytes 294944 | tf_op jit(solution)/shard_map/ppermute | solution.py:21
  73.7 0.4 collective-permute-start.1
  74.1 10.4 %collective-permute-done.1 = bf16[96,2304]{1,0:T(8,128)(2,1)S(1)} collective-permute-done((bf16[96,2304]{1,0:T(8,128)(2,1)S(1)}, bf16[96,2304]{1,0:T(8,128)(2,1)S(1)}, u32[]{:S(2)}, u32[]{:S(2)}) %collective-permute-start.1) | collective-permute-done | bytes 442400 | tf_op jit(solution)/shard_map/ppermute | solution.py:21
  84.5 0.1 collective-permute-start.2
  84.6 0.1 pad_add_fusion.place_ref
  84.7 2.5 %collective-permute-done.2.far_ref = bf16[224,2304]{1,0:T(8,128)(2,1)S(1)} collective-permute-done((bf16[224,2304]{1,0:T(8,128)(2,1)S(1)}, bf16[224,2304]{1,0:T(8,128)(2,1)S(1)}, u32[]{:S(2)}, u32[]{:S(2)}) %collective-permute-start.2) | collective-permute-done | bytes 1032224 | tf_op jit(solution)/shard_map/ppermute | solution.py:21
  87.3 0.0 all-to-all-done
  87.3 21.5 %feed_forward.1 = bf16[512,4096]{1,0:T(8,128)(2,1)} custom-call(s32[2]{0:T(128)S(1)} %pad_add_fusion.place_ref, bf16[512,4096]{1,0:T(8,128)(2,1)} %bitcast.6.x_ref, bf16[4096,768]{1,0:T(8,128)(2,1)} %wg_ref.1, bf16[4096,768]{1,0:T(8,128)(2,1)} %wu_ref.1, bf16[768,4096]{1,0:T(8,128)(2,1)} %wd_ref.1, ...), custom_call_target="tpu_custom_call" | custom-call | flops 9663676416 | bytes 29360128 | tf_op jit(solution)/shard_map/feed_forward/pallas_call | solution.py:179
  108.8 7.4 %all-to-all-start.1 = ((bf16[32,16,4096]{2,1,0:T(8,128)(2,1)}), bf16[32,16,4096]{2,1,0:T(8,128)(2,1)}, u32[]{:S(2)}, u32[]{:S(2)}) async-start(bf16[32,16,4096]{2,1,0:T(8,128)(2,1)} %bitcast.21), calls=%async_computation.1 | async-start | bytes 8388608 | tf_op jit(solution)/shard_map/all_to_all | solution.py:295
  116.2 0.8 dynamic-slice_bitcast_fusion.weight_ref
  116.9 55.2 %all-to-all-done.1 = bf16[32,16,4096]{2,1,0:T(8,128)(2,1)} async-done(((bf16[32,16,4096]{2,1,0:T(8,128)(2,1)}), bf16[32,16,4096]{2,1,0:T(8,128)(2,1)}, u32[]{:S(2)}, u32[]{:S(2)}) %all-to-all-start.1) | async-done | bytes 4194336 | tf_op jit(solution)/shard_map/all_to_all | solution.py:295
  172.1 5.0 %combine.1 = bf16[32,4096]{1,0:T(8,128)(2,1)} custom-call(s32[4,32]{1,0:T(4,128)S(1)} %dynamic-slice_bitcast_fusion.1.route_ref, f32[4,32]{1,0:T(4,128)S(1)} %dynamic-slice_bitcast_fusion.weight_ref, bf16[512,4096]{1,0:T(8,128)(2,1)} %bitcast.12.part_ref), custom_call_target="tpu_custom_call" | custom-call | flops 268435456 | bytes 5242880 | tf_op jit(solution)/shard_map/combine/pallas_call | solution.py:235
  (18 shorter events, 0.2 us)
Async XLA Ops:
  0.0 0.7 copy-start
  0.8 0.9 copy-start.2
  1.7 0.7 copy-start.3
  3.8 2.0 %copy-start.1 = (bf16[16,2,16,4096]{3,2,1,0:T(8,128)(2,1)}, bf16[16,2,16,4096]{3,2,1,0:T(8,128)(2,1)S(1)}, u32[]{:S(2)}) copy-start(bf16[16,2,16,4096]{3,2,1,0:T(8,128)(2,1)S(1)} %dispatch.1) | copy-start | bytes 12582916
  5.8 9.7 %copy-start.4 = (bf16[2,1024,32]{1,2,0:T(8,128)(2,1)S(1)}, bf16[2,1024,32]{1,2,0:T(8,128)(2,1)}, u32[]{:S(2)}) copy-start(bf16[2,1024,32]{1,2,0:T(8,128)(2,1)} %param.18) | copy-start | bytes 393220
  5.8 9.7 %copy-start.7 = (bf16[2,16,768]{2,1,0:T(8,128)(2,1)S(1)}, bf16[2,16,768]{2,1,0:T(8,128)(2,1)}, u32[]{:S(2)}) copy-start(bf16[2,16,768]{2,1,0:T(8,128)(2,1)} %param.19) | copy-start | bytes 147460
  5.8 9.8 %copy-start.6 = (bf16[16,2048]{1,0:T(8,128)(2,1)S(1)}, bf16[16,2048]{1,0:T(8,128)(2,1)}, u32[]{:S(2)}) copy-start(bf16[16,2048]{1,0:T(8,128)(2,1)} %param.21) | copy-start | bytes 196612
  5.8 9.8 %copy-start.5 = (bf16[768,16]{0,1:T(8,128)(2,1)S(1)}, bf16[768,16]{0,1:T(8,128)(2,1)}, u32[]{:S(2)}) copy-start(bf16[768,16]{0,1:T(8,128)(2,1)} %param.20) | copy-start | bytes 73732
  5.8 81.4 %all-to-all-start = ((bf16[32,16,4096]{2,1,0:T(8,128)(2,1)}), bf16[32,16,4096]{2,1,0:T(8,128)(2,1)}, u32[]{:S(2)}, u32[]{:S(2)}) async-start(bf16[32,16,4096]{2,1,0:T(8,128)(2,1)} %bitcast.19), calls=%async_computation | async-start | bytes 8388608 | tf_op jit(solution)/shard_map/all_to_all | solution.py:290
  15.6 58.0 %collective-permute-start = (bf16[64,2304]{1,0:T(8,128)(2,1)S(1)}, bf16[64,2304]{1,0:T(8,128)(2,1)S(1)}, u32[]{:S(2)}, u32[]{:S(2)}) collective-permute-start(bf16[64,2304]{1,0:T(8,128)(2,1)S(1)} %maximum_maximum_fusion), channel_id=1, source_target_pairs={{0,64},{32,96},{64,0},{96,32},{1,65},{33,97},{65,1},{97,33},{2,66}... | collective-permute-start | bytes 884744 | tf_op jit(solution)/shard_map/ppermute | solution.py:21
  73.7 10.8 %collective-permute-start.1 = (bf16[96,2304]{1,0:T(8,128)(2,1)S(1)}, bf16[96,2304]{1,0:T(8,128)(2,1)S(1)}, u32[]{:S(2)}, u32[]{:S(2)}) collective-permute-start(bf16[96,2304]{1,0:T(8,128)(2,1)S(1)} %pad_maximum_fusion), channel_id=1, source_target_pairs={{0,1},{1,0},{2,3},{3,2},{4,5},{5,4},{6,7},{7,6},{8,9},{9,8},{10,11... | collective-permute-start | bytes 1327112 | tf_op jit(solution)/shard_map/ppermute | solution.py:21
  84.5 2.7 %collective-permute-start.2 = (bf16[224,2304]{1,0:T(8,128)(2,1)S(1)}, bf16[224,2304]{1,0:T(8,128)(2,1)S(1)}, u32[]{:S(2)}, u32[]{:S(2)}) collective-permute-start(bf16[224,2304]{1,0:T(8,128)(2,1)S(1)} %constant_dynamic-update-slice_fusion.own_ref), channel_id=1, source_target_pairs={{0,32},{32,0},{64,96},{96,64},{1,33},{33,1},{65,97},{97,65},{2,34}... | collective-permute-start | bytes 3096584 | tf_op jit(solution)/shard_map/ppermute | solution.py:21
  108.8 63.3 %all-to-all-start.1 = ((bf16[32,16,4096]{2,1,0:T(8,128)(2,1)}), bf16[32,16,4096]{2,1,0:T(8,128)(2,1)}, u32[]{:S(2)}, u32[]{:S(2)}) async-start(bf16[32,16,4096]{2,1,0:T(8,128)(2,1)} %bitcast.21), calls=%async_computation.1 | async-start | bytes 8388608 | tf_op jit(solution)/shard_map/all_to_all | solution.py:295

commit v2 on v1

--- a/solution.py
+++ b/solution.py
@@ -11,6 +11,9 @@
 NORM_EPS = 1e-06
 EXPERTS = 16
 CAP = 16
+PART = CAP // 2
+FFN_VMEM = 50 << 20
+DISPATCH_VMEM = 60 << 20
 F32 = jnp.float32
 BF16 = jnp.bfloat16
 NT = (((1,), (1,)), ((), ()))
@@ -21,7 +24,7 @@
     return lax.ppermute(value, axis, [(i, i ^ bit) for i in range(lax.axis_size(axis))])
 
 
-def slots_of(route_t, copies):
+def slots_of(route_t, depth, copies, first):
     rows = route_t.shape[1]
     experts = lax.broadcasted_iota(jnp.int32, (EXPERTS, rows), 0)
     chosen = jnp.zeros((EXPERTS, rows), jnp.bool_)
@@ -33,11 +36,11 @@
     ).astype(F32)
     place = jnp.dot(chosen.astype(F32), upper, preferred_element_type=F32).astype(jnp.int32) - 1
     place = jnp.where(chosen, place, -1)
-    slot = lax.broadcasted_iota(jnp.int32, (EXPERTS, copies * CAP, rows), 1) % CAP
-    return place[:, None, :] == slot
-
-
-def dispatch_body(tokens_ref, gain_ref, route_ref, out_ref, normed_ref, mask_ref):
+    slot = lax.broadcasted_iota(jnp.int32, (EXPERTS, copies * depth, rows), 1) % depth
+    return place[:, None, :] == slot + first
+
+
+def dispatch_body(tokens_ref, gain_ref, route_ref, early_ref, late_ref, normed_ref, mask_ref):
     step = pl.program_id(0)
 
     @pl.when(step == 0)
@@ -45,33 +48,36 @@
         wide = tokens_ref[...].astype(F32)
         spread = jnp.mean(wide * wide, axis=-1, keepdims=True)
         normed_ref[...] = (wide * lax.rsqrt(spread + NORM_EPS) * gain_ref[...]).astype(BF16)
-        mask = slots_of(route_ref[...], 1)
+        mask = slots_of(route_ref[...], CAP, 1, 0)
         mask_ref[...] = mask.astype(F32).reshape(EXPERTS * CAP, -1).astype(BF16)
 
-    per = out_ref.shape[0]
+    per = early_ref.shape[0]
     pick = mask_ref[pl.ds(pl.multiple_of(step * per * CAP, per * CAP), per * CAP), :]
-    rows = jnp.dot(pick, normed_ref[...], preferred_element_type=F32).astype(BF16)
+    rows = jnp.dot(pick, normed_ref[...], preferred_element_type=F32)
     for i in range(per):
-        out_ref[i, 0] = rows[i * CAP : (i + 1) * CAP]
-        out_ref[i, 1] = rows[i * CAP : (i + 1) * CAP]
+        for half in range(2):
+            early_ref[i, half] = rows[i * CAP : i * CAP + PART].astype(BF16)
+            late_ref[i, half] = rows[i * CAP + PART : (i + 1) * CAP].astype(BF16)
 
 
 def dispatch(tokens, gain, route_t):
     rows, width = tokens.shape
     steps = 4
     per = EXPERTS // steps
+    sent = pltpu.HBM((EXPERTS, 2, PART, width), BF16)
+    out_spec = pl.BlockSpec((per, 2, PART, width), lambda i: (i, 0, 0, 0))
     return pl.pallas_call(
         dispatch_body,
         grid=(steps,),
-        out_shape=jax.ShapeDtypeStruct((EXPERTS, 2, CAP, width), BF16),
+        out_shape=(sent, sent),
         in_specs=[
             pl.BlockSpec((rows, width), lambda i: (0, 0)),
             pl.BlockSpec((1, width), lambda i: (0, 0)),
             pl.BlockSpec(route_t.shape, lambda i: (0, 0)),
         ],
-        out_specs=pl.BlockSpec((per, 2, CAP, width), lambda i: (i, 0, 0, 0)),
+        out_specs=(out_spec, out_spec),
         scratch_shapes=[pltpu.VMEM((rows, width), BF16), pltpu.VMEM((EXPERTS * CAP, rows), BF16)],
-        compiler_params=pltpu.CompilerParams(vmem_limit_bytes=24 << 20),
+        compiler_params=pltpu.CompilerParams(vmem_limit_bytes=DISPATCH_VMEM),
         cost_estimate=pl.CostEstimate(
             flops=2 * EXPERTS * CAP * rows * width, bytes_accessed=5 << 20, transcendentals=0
         ),
@@ -198,8 +204,8 @@
                 pltpu.VMEM((2, 64, width // 2), BF16),
             ],
         ),
-        out_shape=jax.ShapeDtypeStruct((rows, width), BF16),
-        compiler_params=pltpu.CompilerParams(vmem_limit_bytes=48 << 20),
+        out_shape=pltpu.HBM((rows, width), BF16),
+        compiler_params=pltpu.CompilerParams(vmem_limit_bytes=FFN_VMEM),
         cost_estimate=pl.CostEstimate(
             flops=6 * rows * width * hidden, bytes_accessed=28 << 20, transcendentals=rows * hidden
         ),
@@ -207,7 +213,10 @@
     )(place, x, wg, wu, wd, own, far)
 
 
-def combine_body(route_ref, weight_ref, part_ref, out_ref, high_ref, low_ref):
+def combine_body(first, route_ref, weight_ref, part_ref, *refs):
+    base_ref = refs[0] if len(refs) == 4 else None
+    out_ref, high_ref, low_ref = refs[-3:]
+
     @pl.when(pl.program_id(0) == 0)
     def _():
         route_t, weight_t = route_ref[...], weight_ref[...]
@@ -216,8 +225,8 @@
         weight = jnp.zeros((EXPERTS, rows), F32)
         for k in range(route_t.shape[0]):
             weight += jnp.where(route_t[k : k + 1, :] == experts, weight_t[k : k + 1, :], 0.0)
-        mask = slots_of(route_t, 2)
-        spread = jnp.where(mask, weight[:, None, :], 0.0).reshape(2 * EXPERTS * CAP, rows)
+        mask = slots_of(route_t, PART, 2, first)
+        spread = jnp.where(mask, weight[:, None, :], 0.0).reshape(2 * EXPERTS * PART, rows)
         high = spread.astype(BF16)
         high_ref[...] = high
         low_ref[...] = (spread - high.astype(F32)).astype(BF16)
@@ -225,30 +234,38 @@
     part = part_ref[...]
     total = lax.dot_general(high_ref[...], part, TN, preferred_element_type=F32)
     total += lax.dot_general(low_ref[...], part, TN, preferred_element_type=F32)
-    out_ref[...] = total.astype(BF16)
-
-
-def combine(route_t, weight_t, part):
+    if base_ref is not None:
+        total += base_ref[...]
+    out_ref[...] = total.astype(out_ref.dtype)
+
+
+def combine(route_t, weight_t, part, first, base, out_type):
     slots, width = part.shape
     rows = route_t.shape[1]
     cols = 1024
+    sheet = pl.BlockSpec((rows, cols), lambda i: (0, i))
+    in_specs = [
+        pl.BlockSpec(route_t.shape, lambda i: (0, 0)),
+        pl.BlockSpec(weight_t.shape, lambda i: (0, 0)),
+        pl.BlockSpec((slots, cols), lambda i: (0, i)),
+    ]
+    operands = (route_t, weight_t, part)
+    if base is not None:
+        in_specs.append(sheet)
+        operands += (base,)
     return pl.pallas_call(
-        combine_body,
+        functools.partial(combine_body, first),
         grid=(width // cols,),
-        out_shape=jax.ShapeDtypeStruct((rows, width), BF16),
-        in_specs=[
-            pl.BlockSpec(route_t.shape, lambda i: (0, 0)),
-            pl.BlockSpec(weight_t.shape, lambda i: (0, 0)),
-            pl.BlockSpec((slots, cols), lambda i: (0, i)),
-        ],
-        out_specs=pl.BlockSpec((rows, cols), lambda i: (0, i)),
+        out_shape=jax.ShapeDtypeStruct((rows, width), out_type),
+        in_specs=in_specs,
+        out_specs=sheet,
         scratch_shapes=[pltpu.VMEM((slots, rows), BF16), pltpu.VMEM((slots, rows), BF16)],
         compiler_params=pltpu.CompilerParams(vmem_limit_bytes=24 << 20),
         cost_estimate=pl.CostEstimate(
-            flops=4 * slots * rows * width, bytes_accessed=5 << 20, transcendentals=0
+            flops=4 * slots * rows * width, bytes_accessed=3 << 20, transcendentals=0
         ),
         name="combine",
-    )(route_t, weight_t, part)
+    )(*operands)
 
 
 def gather_factors(input_left, input_right, output_left, output_right):
@@ -258,10 +275,14 @@
     pad = lambda a: jnp.pad(a, ((0, 0), (0, wide - a.shape[1])))
     mine = jnp.concatenate([pad(left), pad(output_right), right], axis=0)
     shared = left.shape[0] + output_right.shape[0]
+    groups, tensor = lax.axis_size("group"), lax.axis_size("tensor")
+    both = [
+        (g * tensor + t, (g ^ 2) * tensor + (t ^ 1)) for g in range(groups) for t in range(tensor)
+    ]
     across_x = exchange(mine, "group", 2)
-    partner = exchange(jnp.concatenate([mine[:shared], across_x[:shared]], axis=0), "tensor", 1)
-    own = jnp.concatenate([mine, across_x, partner], axis=0)
-    return own, exchange(own, "group", 1)
+    partner = exchange(mine[:shared], "tensor", 1)
+    corner = lax.ppermute(mine[:shared], ("group", "tensor"), both)
+    return mine, across_x, partner, corner
 
 
 def on_device(
@@ -280,20 +301,25 @@
     rows, width = tokens.shape
     position = lax.axis_index("tensor")
     place = jnp.stack([lax.axis_index("group"), position % 2]).astype(jnp.int32)
-    own, far = gather_factors(
+    pieces = gather_factors(
         adapter_input_left, adapter_input_right, adapter_output_left, adapter_output_right
     )
     route_t = lax.dynamic_slice_in_dim(routing, position * rows, rows, 0).T
     weight_t = lax.dynamic_slice_in_dim(chosen_expert_weights, position * rows, rows, 0).T
     sent = dispatch(tokens, expert_norm_gain.reshape(1, width), route_t)
-    sent = sent.reshape(2 * EXPERTS, CAP, width)
-    x = lax.all_to_all(sent, "tensor", 0, 0, tiled=True).reshape(2 * EXPERTS * CAP, width)
-    part = feed_forward(
-        place, x, resident_gate_weight, resident_up_weight, resident_down_weight, own, far
-    )
-    part = part.reshape(2 * EXPERTS, CAP, width)
-    back = lax.all_to_all(part, "tensor", 0, 0, tiled=True).reshape(2 * EXPERTS * CAP, width)
-    return combine(route_t, weight_t, back)
+
+    def travel(value):
+        value = value.reshape(2 * EXPERTS, PART, width)
+        return lax.all_to_all(value, "tensor", 0, 0, tiled=True).reshape(-1, width)
+
+    weights = (resident_gate_weight, resident_up_weight, resident_down_weight)
+    arrived = [travel(value) for value in sent]
+    *pieces, arrived[0] = lax.optimization_barrier((*pieces, arrived[0]))
+    own = jnp.concatenate(pieces, axis=0)
+    far = exchange(own, "group", 1)
+    parts = [travel(feed_forward(place, x, *weights, own, far)) for x in arrived]
+    base = combine(route_t, weight_t, parts[0], 0, None, F32)
+    return combine(route_t, weight_t, parts[1], PART, base, BF16)
 
 
 def solution(mesh):

time: 178 us -> 151 us (0.85)
  waiting for transfers between devices: 124 us -> 72.7 us
  Pallas kernels: 27.9 us -> 42.1 us
  starting transfers between devices: 19.8 us -> 30.7 us
    ppermute x3, waiting for transfers between devices: 68.7 us -> 2.54 us  [exchange(): lax.ppermute(value, axis, [(i, i ^ bit) for i in range(lax.axis_size(axis...]
    all_to_all x2 -> x4, waiting for transfers between devices: 55.2 us -> 67.1 us  [travel(): return lax.all_to_all(value, 'tensor', 0, 0, tiled=True).reshape(-1, width)]
    pallas_call x1 -> x2, Pallas kernels: 21.5 us -> 32.2 us  [feed_forward(): pl.pallas_call(functools.partial(ffn_body, hid_steps), grid_spec=pltpu.Pr...]
    all_to_all x2 -> x4, starting transfers between devices: 17 us -> 25.5 us  [travel(): return lax.all_to_all(value, 'tensor', 0, 0, tiled=True).reshape(-1, width)]
    pallas_call x2 -> x3, Pallas kernels: 6.36 us -> 9.9 us  [the longest x2 5.81 us: combine(): pl.pallas_call(functools.partial(combine_body, first), grid=(width // col...]
    ppermute x0 -> x1, waiting for transfers between devices: none -> 3.07 us  [gather_factors(): corner = lax.ppermute(mine[:shared], ('group', 'tensor'), both)]
    ppermute x0 -> x1, starting transfers between devices: none -> 2.39 us  [gather_factors(): corner = lax.ppermute(mine[:shared], ('group', 'tensor'), both)]
    unnamed x17 -> x21, local copies, waits for them, and re-layouts: 4.39 us -> 3.36 us
  transfers between devices with their start and end apart: 5 -> 8, of which waited for: 4 -> 6; matrix products, arithmetic and copies ran while one was open for 1% -> 1% of each run, Pallas kernels for 0% -> 22%
where the time goes in v2:
time: 151 us
  waiting for transfers between devices  72.7 us (48%)
  Pallas kernels  42.1 us (28%)
  starting transfers between devices  30.7 us (20%)
  local copies, waits for them, and re-layouts  4.82 us (3%)
    all_to_all x4, waiting for transfers between devices, travel(): return lax.all_to_all(value, 'tensor', 0, 0, tiled=True).reshape(-1, width)  67.1 us
    pallas_call x2, Pallas kernels, feed_forward(): pl.pallas_call(functools.partial(ffn_body, hid_steps), grid_spec=pltpu.Pr...  32.2 us
    all_to_all x4, starting transfers between devices, travel(): return lax.all_to_all(value, 'tensor', 0, 0, tiled=True).reshape(-1, width)  25.5 us
    pallas_call x2, Pallas kernels, combine(): pl.pallas_call(functools.partial(combine_body, first), grid=(width // col...  5.81 us
    pallas_call x1, Pallas kernels, dispatch(): pl.pallas_call(dispatch_body, grid=(steps,), out_shape=(sent, sent), in_s...  4.09 us
    unnamed x21, local copies, waits for them, and re-layouts  3.36 us
    ppermute x1, waiting for transfers between devices, gather_factors(): corner = lax.ppermute(mine[:shared], ('group', 'tensor'), both)  3.07 us
  transfers between devices with their start and end apart: 8, of which 6 were waited for; matrix products, arithmetic and copies ran while one was open for 1% of the time, Pallas kernels for 22%

profile of v2, /device:TPU:10, one launch (start us, length us, event | category | flops | bytes accessed | tf_op | source)
XLA Modules:
  0.0 150.7 jit_solution(4844409930835059089)
XLA Ops:
  0.0 0.7 copy-done
  0.7 0.6 dynamic-slice_bitcast_fusion.1.route_ref
  1.4 4.1 %dispatch.1 = (bf16[16,2,8,4096]{3,2,1,0:T(8,128)(2,1)}, bf16[16,2,8,4096]{3,2,1,0:T(8,128)(2,1)}) custom-call(bf16[32,4096]{1,0:T(8,128)(2,1)} %tokens_ref.1, f32[1,4096]{1,0:T(1,128)} %bitcast.32, s32[4,32]{1,0:T(4,128)} %dynamic-slice_bitcast_fusion.1.route_ref), custom_call_target="tpu_custom_call" | custom-call | flops 67108864 | bytes 5242880 | tf_op jit(solution)/shard_map/dispatch/pallas_call | solution.py:69
  5.5 9.6 %all-to-all-start.1 = ((bf16[32,8,4096]{2,1,0:T(8,128)(2,1)}), bf16[32,8,4096]{2,1,0:T(8,128)(2,1)S(1)}, u32[]{:S(2)}, u32[]{:S(2)}) async-start(bf16[32,8,4096]{2,1,0:T(8,128)(2,1)} %bitcast.28), calls=%async_computation.1 | async-start | bytes 4194304 | tf_op jit(solution)/shard_map/all_to_all | solution.py:313
  15.2 2.2 %collective-permute-start = (bf16[64,2304]{1,0:T(8,128)(2,1)S(1)}, bf16[64,2304]{1,0:T(8,128)(2,1)S(1)}, u32[]{:S(2)}, u32[]{:S(2)}) collective-permute-start(bf16[64,2304]{1,0:T(8,128)(2,1)S(1)} %maximum_maximum_fusion), channel_id=1, source_target_pairs={{0,64},{32,96},{64,0},{96,32},{1,65},{33,97},{65,1},{97,33},{2,66}... | collective-permute-start | bytes 884744 | tf_op jit(solution)/shard_map/ppermute | solution.py:24
  17.5 2.4 %collective-permute-start.2 = (bf16[48,2304]{1,0:T(8,128)(2,1)S(1)}, bf16[48,2304]{1,0:T(8,128)(2,1)S(1)}, u32[]{:S(2)}, u32[]{:S(2)}) collective-permute-start(bf16[48,2304]{1,0:T(8,128)(2,1)S(1)} %pad_maximum_fusion), channel_id=1, source_target_pairs={{0,65},{1,64},{2,67},{3,66},{4,69},{5,68},{6,71},{7,70},{8,73},{9,... | collective-permute-start | bytes 663560 | tf_op jit(solution)/shard_map/ppermute | solution.py:284
  19.8 0.6 collective-permute-start.1
  20.4 23.2 %all-to-all-done.1 = bf16[32,8,4096]{2,1,0:T(8,128)(2,1)S(1)} async-done(((bf16[32,8,4096]{2,1,0:T(8,128)(2,1)}), bf16[32,8,4096]{2,1,0:T(8,128)(2,1)S(1)}, u32[]{:S(2)}, u32[]{:S(2)}) %all-to-all-start.1) | async-done | bytes 2097184 | tf_op jit(solution)/shard_map/all_to_all | solution.py:313
  43.7 1.3 copy-done.4
  45.0 5.0 %all-to-all-start = ((bf16[32,8,4096]{2,1,0:T(8,128)(2,1)}), bf16[32,8,4096]{2,1,0:T(8,128)(2,1)}, u32[]{:S(2)}, u32[]{:S(2)}) async-start(bf16[32,8,4096]{2,1,0:T(8,128)(2,1)} %bitcast.27), calls=%async_computation | async-start | bytes 4194304 | tf_op jit(solution)/shard_map/all_to_all | solution.py:313
  50.0 3.1 %collective-permute-done.2 = bf16[48,2304]{1,0:T(8,128)(2,1)S(1)} collective-permute-done((bf16[48,2304]{1,0:T(8,128)(2,1)S(1)}, bf16[48,2304]{1,0:T(8,128)(2,1)S(1)}, u32[]{:S(2)}, u32[]{:S(2)}) %collective-permute-start.2) | collective-permute-done | bytes 221216 | tf_op jit(solution)/shard_map/ppermute | solution.py:284
  53.2 0.1 collective-permute-start.3
  53.3 2.5 %collective-permute-done.3.far_ref = bf16[224,2304]{1,0:T(8,128)(2,1)S(1)} collective-permute-done((bf16[224,2304]{1,0:T(8,128)(2,1)S(1)}, bf16[224,2304]{1,0:T(8,128)(2,1)S(1)}, u32[]{:S(2)}, u32[]{:S(2)}) %collective-permute-start.3) | collective-permute-done | bytes 1032224 | tf_op jit(solution)/shard_map/ppermute | solution.py:24
  55.9 16.1 %feed_forward.3 = bf16[256,4096]{1,0:T(8,128)(2,1)} custom-call(s32[2]{0:T(128)S(1)} %pad_add_fusion.place_ref, bf16[256,4096]{1,0:T(8,128)(2,1)} %bitcast.24, bf16[4096,768]{1,0:T(8,128)(2,1)} %wg_ref.3, bf16[4096,768]{1,0:T(8,128)(2,1)} %wu_ref.3, bf16[768,4096]{1,0:T(8,128)(2,1)} %wd_ref.3, ...), custom_call_target="tpu_custom_call" | custom-call | flops 4831838208 | bytes 29360128 | tf_op jit(solution)/shard_map/feed_forward/pallas_call | solution.py:185
  72.0 5.7 %all-to-all-done = bf16[32,8,4096]{2,1,0:T(8,128)(2,1)} async-done(((bf16[32,8,4096]{2,1,0:T(8,128)(2,1)}), bf16[32,8,4096]{2,1,0:T(8,128)(2,1)}, u32[]{:S(2)}, u32[]{:S(2)}) %all-to-all-start) | async-done | bytes 2097184 | tf_op jit(solution)/shard_map/all_to_all | solution.py:313
  77.7 5.9 %all-to-all-start.3 = ((bf16[32,8,4096]{2,1,0:T(8,128)(2,1)}), bf16[32,8,4096]{2,1,0:T(8,128)(2,1)S(1)}, u32[]{:S(2)}, u32[]{:S(2)}) async-start(bf16[32,8,4096]{2,1,0:T(8,128)(2,1)} %bitcast.26), calls=%async_computation.3 | async-start | bytes 4194304 | tf_op jit(solution)/shard_map/all_to_all | solution.py:313
  83.6 1.2 copy-done.2
  84.8 16.0 %feed_forward.2 = bf16[256,4096]{1,0:T(8,128)(2,1)} custom-call(s32[2]{0:T(128)S(1)} %pad_add_fusion.place_ref, bf16[256,4096]{1,0:T(8,128)(2,1)} %bitcast.6.x_ref, bf16[4096,768]{1,0:T(8,128)(2,1)} %wg_ref.3, bf16[4096,768]{1,0:T(8,128)(2,1)} %wu_ref.3, bf16[768,4096]{1,0:T(8,128)(2,1)} %wd_ref.3, ...), custom_call_target="tpu_custom_call" | custom-call | flops 4831838208 | bytes 29360128 | tf_op jit(solution)/shard_map/feed_forward/pallas_call | solution.py:185
  100.9 11.6 %all-to-all-done.3 = bf16[32,8,4096]{2,1,0:T(8,128)(2,1)S(1)} async-done(((bf16[32,8,4096]{2,1,0:T(8,128)(2,1)}), bf16[32,8,4096]{2,1,0:T(8,128)(2,1)S(1)}, u32[]{:S(2)}, u32[]{:S(2)}) %all-to-all-start.3) | async-done | bytes 2097184 | tf_op jit(solution)/shard_map/all_to_all | solution.py:313
  112.5 5.0 %all-to-all-start.2 = ((bf16[32,8,4096]{2,1,0:T(8,128)(2,1)}), bf16[32,8,4096]{2,1,0:T(8,128)(2,1)}, u32[]{:S(2)}, u32[]{:S(2)}) async-start(bf16[32,8,4096]{2,1,0:T(8,128)(2,1)} %bitcast.25), calls=%async_computation.2 | async-start | bytes 4194304 | tf_op jit(solution)/shard_map/all_to_all | solution.py:313
  117.5 0.8 dynamic-slice_bitcast_fusion.weight_ref
  118.3 1.6 %combine.2.refs_0_ = f32[32,4096]{1,0:T(8,128)S(1)} custom-call(s32[4,32]{1,0:T(4,128)S(1)} %copy-done.3, f32[4,32]{1,0:T(4,128)S(1)} %dynamic-slice_bitcast_fusion.weight_ref, bf16[256,4096]{1,0:T(8,128)(2,1)S(1)} %bitcast.23), custom_call_target="tpu_custom_call" | custom-call | flops 134217728 | bytes 3145728 | tf_op jit(solution)/shard_map/combine/pallas_call | solution.py:256
  119.9 26.5 %all-to-all-done.2 = bf16[32,8,4096]{2,1,0:T(8,128)(2,1)} async-done(((bf16[32,8,4096]{2,1,0:T(8,128)(2,1)}), bf16[32,8,4096]{2,1,0:T(8,128)(2,1)}, u32[]{:S(2)}, u32[]{:S(2)}) %all-to-all-start.2) | async-done | bytes 2097184 | tf_op jit(solution)/shard_map/all_to_all | solution.py:313
  146.5 4.2 %combine.3 = bf16[32,4096]{1,0:T(8,128)(2,1)} custom-call(s32[4,32]{1,0:T(4,128)S(1)} %copy-done.3, f32[4,32]{1,0:T(4,128)S(1)} %dynamic-slice_bitcast_fusion.weight_ref, bf16[256,4096]{1,0:T(8,128)(2,1)} %bitcast.14.part_ref, f32[32,4096]{1,0:T(8,128)S(1)} %combine.2.refs_0_), custom_call_target="tpu_custom_call" | custom-call | flops 134217728 | bytes 3145728 | tf_op jit(solution)/shard_map/combine/pallas_call | solution.py:256
  (28 shorter events, 0.3 us)
Async XLA Ops:
  0.0 0.7 copy-start
  5.5 9.6 %copy-start.5 = (bf16[2,1024,32]{1,2,0:T(8,128)(2,1)S(1)}, bf16[2,1024,32]{1,2,0:T(8,128)(2,1)}, u32[]{:S(2)}) copy-start(bf16[2,1024,32]{1,2,0:T(8,128)(2,1)} %param.18) | copy-start | bytes 393220
  5.5 9.7 %copy-start.6 = (bf16[16,2048]{1,0:T(8,128)(2,1)S(1)}, bf16[16,2048]{1,0:T(8,128)(2,1)}, u32[]{:S(2)}) copy-start(bf16[16,2048]{1,0:T(8,128)(2,1)} %param.21) | copy-start | bytes 196612
  5.5 9.7 %copy-start.7 = (bf16[2,16,768]{2,1,0:T(8,128)(2,1)S(1)}, bf16[2,16,768]{2,1,0:T(8,128)(2,1)}, u32[]{:S(2)}) copy-start(bf16[2,16,768]{2,1,0:T(8,128)(2,1)} %param.19) | copy-start | bytes 147460
  5.5 9.7 %copy-start.8 = (bf16[768,16]{0,1:T(8,128)(2,1)S(1)}, bf16[768,16]{0,1:T(8,128)(2,1)}, u32[]{:S(2)}) copy-start(bf16[768,16]{0,1:T(8,128)(2,1)} %param.20) | copy-start | bytes 73732
  5.5 38.2 %all-to-all-start.1 = ((bf16[32,8,4096]{2,1,0:T(8,128)(2,1)}), bf16[32,8,4096]{2,1,0:T(8,128)(2,1)S(1)}, u32[]{:S(2)}, u32[]{:S(2)}) async-start(bf16[32,8,4096]{2,1,0:T(8,128)(2,1)} %bitcast.28), calls=%async_computation.1 | async-start | bytes 4194304 | tf_op jit(solution)/shard_map/all_to_all | solution.py:313
  15.2 37.8 %collective-permute-start = (bf16[64,2304]{1,0:T(8,128)(2,1)S(1)}, bf16[64,2304]{1,0:T(8,128)(2,1)S(1)}, u32[]{:S(2)}, u32[]{:S(2)}) collective-permute-start(bf16[64,2304]{1,0:T(8,128)(2,1)S(1)} %maximum_maximum_fusion), channel_id=1, source_target_pairs={{0,64},{32,96},{64,0},{96,32},{1,65},{33,97},{65,1},{97,33},{2,66}... | collective-permute-start | bytes 884744 | tf_op jit(solution)/shard_map/ppermute | solution.py:24
  17.5 35.6 %collective-permute-start.2 = (bf16[48,2304]{1,0:T(8,128)(2,1)S(1)}, bf16[48,2304]{1,0:T(8,128)(2,1)S(1)}, u32[]{:S(2)}, u32[]{:S(2)}) collective-permute-start(bf16[48,2304]{1,0:T(8,128)(2,1)S(1)} %pad_maximum_fusion), channel_id=1, source_target_pairs={{0,65},{1,64},{2,67},{3,66},{4,69},{5,68},{6,71},{7,70},{8,73},{9,... | collective-permute-start | bytes 663560 | tf_op jit(solution)/shard_map/ppermute | solution.py:284
  19.8 33.2 %collective-permute-start.1 = (bf16[48,2304]{1,0:T(8,128)(2,1)S(1)}, bf16[48,2304]{1,0:T(8,128)(2,1)S(1)}, u32[]{:S(2)}, u32[]{:S(2)}) collective-permute-start(bf16[48,2304]{1,0:T(8,128)(2,1)S(1)} %pad_maximum_fusion), channel_id=1, source_target_pairs={{0,1},{1,0},{2,3},{3,2},{4,5},{5,4},{6,7},{7,6},{8,9},{9,8},{10,11... | collective-permute-start | bytes 663560 | tf_op jit(solution)/shard_map/ppermute | solution.py:24
  43.6 1.3 copy-start.4
  45.0 32.7 %all-to-all-start = ((bf16[32,8,4096]{2,1,0:T(8,128)(2,1)}), bf16[32,8,4096]{2,1,0:T(8,128)(2,1)}, u32[]{:S(2)}, u32[]{:S(2)}) async-start(bf16[32,8,4096]{2,1,0:T(8,128)(2,1)} %bitcast.27), calls=%async_computation | async-start | bytes 4194304 | tf_op jit(solution)/shard_map/all_to_all | solution.py:313
  53.2 2.7 %collective-permute-start.3 = (bf16[224,2304]{1,0:T(8,128)(2,1)S(1)}, bf16[224,2304]{1,0:T(8,128)(2,1)S(1)}, u32[]{:S(2)}, u32[]{:S(2)}) collective-permute-start(bf16[224,2304]{1,0:T(8,128)(2,1)S(1)} %constant_dynamic-update-slice_fusion.own_ref), channel_id=1, source_target_pairs={{0,32},{32,0},{64,96},{96,64},{1,33},{33,1},{65,97},{97,65},{2,34}... | collective-permute-start | bytes 3096584 | tf_op jit(solution)/shard_map/ppermute | solution.py:24
  55.9 16.1 %copy-start.1 = (bf16[224,2304]{1,0:T(8,128)(2,1)}, bf16[224,2304]{1,0:T(8,128)(2,1)S(1)}, u32[]{:S(2)}) copy-start(bf16[224,2304]{1,0:T(8,128)(2,1)S(1)} %collective-permute-done.3.far_ref) | copy-start | bytes 3096580
  77.7 34.9 %all-to-all-start.3 = ((bf16[32,8,4096]{2,1,0:T(8,128)(2,1)}), bf16[32,8,4096]{2,1,0:T(8,128)(2,1)S(1)}, u32[]{:S(2)}, u32[]{:S(2)}) async-start(bf16[32,8,4096]{2,1,0:T(8,128)(2,1)} %bitcast.26), calls=%async_computation.3 | async-start | bytes 4194304 | tf_op jit(solution)/shard_map/all_to_all | solution.py:313
  83.6 1.2 copy-start.2
  112.5 5.7 %copy-start.3 = (s32[4,32]{1,0:T(4,128)S(1)}, s32[4,32]{1,0:T(4,128)}, u32[]{:S(2)}) copy-start(s32[4,32]{1,0:T(4,128)} %dynamic-slice_bitcast_fusion.1.route_ref) | copy-start | bytes 1540
  112.5 33.9 %all-to-all-start.2 = ((bf16[32,8,4096]{2,1,0:T(8,128)(2,1)}), bf16[32,8,4096]{2,1,0:T(8,128)(2,1)}, u32[]{:S(2)}, u32[]{:S(2)}) async-start(bf16[32,8,4096]{2,1,0:T(8,128)(2,1)} %bitcast.25), calls=%async_computation.2 | async-start | bytes 4194304 | tf_op jit(solution)/shard_map/all_to_all | solution.py:313

commit v3 on v2

v3 whole, which is shorter than its diff:
```python
import functools

import jax
import jax.numpy as jnp
from jax import lax
from jax.experimental import pallas as pl
from jax.experimental.pallas import tpu as pltpu
from jax.sharding import PartitionSpec as P

ADAPTER_SCALE = 0.5
NORM_EPS = 1e-06
EXPERTS = 16
CAP = 16
PART = CAP // 2
FFN_VMEM = (50 << 20, 62 << 20)
ROWS_AT = ((0, 128), (64, 176))
DISPATCH_VMEM = 64 << 20
F32 = jnp.float32
BF16 = jnp.bfloat16
NT = (((1,), (1,)), ((), ()))
TN = (((0,), (0,)), ((), ()))


def exchange(value, axis, bit):
    return lax.ppermute(value, axis, [(i, i ^ bit) for i in range(lax.axis_size(axis))])


def own_rows(table_ref, rows):
    position = lax.axis_index("tensor")
    per = 128 // rows
    start = pl.multiple_of((position // per) * 128, 128)
    block = table_ref[:, pl.ds(start, 128)]
    return pltpu.roll(block, (128 - (position % per) * rows) % 128, 1)[:, 0:rows]


def slots_of(route_t, depth, copies, first):
    rows = route_t.shape[1]
    experts = lax.broadcasted_iota(jnp.int32, (EXPERTS, rows), 0)
    chosen = jnp.zeros((EXPERTS, rows), jnp.bool_)
    for k in range(route_t.shape[0]):
        chosen = chosen | (route_t[k : k + 1, :] == experts)
    upper = (
        lax.broadcasted_iota(jnp.int32, (rows, rows), 0)
        <= lax.broadcasted_iota(jnp.int32, (rows, rows), 1)
    ).astype(F32)
    place = jnp.dot(chosen.astype(F32), upper, preferred_element_type=F32).astype(jnp.int32) - 1
    place = jnp.where(chosen, place, -1)
    slot = lax.broadcasted_iota(jnp.int32, (EXPERTS, copies * depth, rows), 1) % depth
    return place[:, None, :] == slot + first


def dispatch_body(first, tokens_ref, gain_ref, route_ref, out_ref, normed_ref, mask_ref):
    step = pl.program_id(0)

    @pl.when(step == 0)
    def _():
        wide = tokens_ref[...].astype(F32)
        spread = jnp.mean(wide * wide, axis=-1, keepdims=True)
        normed_ref[...] = (wide * lax.rsqrt(spread + NORM_EPS) * gain_ref[...]).astype(BF16)
        mask = slots_of(own_rows(route_ref, tokens_ref.shape[0]), PART, 1, first)
        mask_ref[...] = mask.astype(F32).reshape(EXPERTS * PART, -1).astype(BF16)

    per = out_ref.shape[0]
    pick = mask_ref[pl.ds(pl.multiple_of(step * per * PART, per * PART), per * PART), :]
    rows = jnp.dot(pick, normed_ref[...], preferred_element_type=F32)
    for i in range(per):
        for half in range(2):
            out_ref[i, half] = rows[i * PART : (i + 1) * PART].astype(BF16)


def dispatch(tokens, gain, route_t, first):
    rows, width = tokens.shape
    steps = 4
    per = EXPERTS // steps
    return pl.pallas_call(
        functools.partial(dispatch_body, first),
        grid=(steps,),
        out_shape=pltpu.HBM((EXPERTS, 2, PART, width), BF16),
        in_specs=[
            pl.BlockSpec((rows, width), lambda i: (0, 0)),
            pl.BlockSpec((1, width), lambda i: (0, 0)),
            pl.BlockSpec(route_t.shape, lambda i: (0, 0)),
        ],
        out_specs=pl.BlockSpec((per, 2, PART, width), lambda i: (i, 0, 0, 0)),
        scratch_shapes=[pltpu.VMEM((rows, width), BF16), pltpu.VMEM((EXPERTS * PART, rows), BF16)],
        compiler_params=pltpu.CompilerParams(vmem_limit_bytes=DISPATCH_VMEM),
        cost_estimate=pl.CostEstimate(
            flops=2 * EXPERTS * PART * rows * width, bytes_accessed=3 << 20, transcendentals=0
        ),
        name="dispatch",
    )(tokens, gain, route_t)


def mixing_body(rows, route_ref, weight_ref, out_ref):
    route_t, weight_t = own_rows(route_ref, rows), own_rows(weight_ref, rows)
    experts = lax.broadcasted_iota(jnp.int32, (EXPERTS, rows), 0)
    weight = jnp.zeros((EXPERTS, rows), F32)
    for k in range(route_t.shape[0]):
        weight += jnp.where(route_t[k : k + 1, :] == experts, weight_t[k : k + 1, :], 0.0)
    for part in range(CAP // PART):
        mask = slots_of(route_t, PART, 2, part * PART)
        spread = jnp.where(mask, weight[:, None, :], 0.0).reshape(2 * EXPERTS * PART, rows).T
        high = spread.astype(BF16)
        out_ref[part, 0:rows, :] = high
        out_ref[part, rows : 2 * rows, :] = (spread - high.astype(F32)).astype(BF16)


def mixing(route_t, weight_t, rows):
    vmem = pl.BlockSpec(memory_space=pltpu.VMEM)
    return pl.pallas_call(
        functools.partial(mixing_body, rows),
        in_specs=[vmem, vmem],
        out_specs=vmem,
        out_shape=jax.ShapeDtypeStruct((CAP // PART, 2 * rows, 2 * EXPERTS * PART), BF16),
        cost_estimate=pl.CostEstimate(flops=1 << 20, bytes_accessed=1 << 17, transcendentals=0),
        name="mixing",
    )(route_t, weight_t)


def ffn_body(
    place_ref, x_ref, wg_ref, wu_ref, wd_ref, own_ref, far_ref, out_ref,
    gate_ref, up_ref, low_ref, right_ref, hidden_ref, mid_ref, outr_ref,
):
    step = pl.program_id(0)
    group, half = place_ref[0], place_ref[1]
    width = hidden_ref.shape[1]
    span = x_ref.shape[1]
    packs = (own_ref, far_ref)

    for turn in range(4):

        @pl.when(step == turn)
        def _(turn=turn):
            xh, pack = turn // 2, packs[turn % 2]
            there = group ^ turn
            near, across = ROWS_AT[xh]
            x = x_ref[...]
            left = jnp.concatenate(
                [
                    pack[near : near + 32, 0:span],
                    pack[near : near + 32, span : 2 * span],
                    pack[across : across + 32, 0:span],
                    pack[across : across + 32, span : 2 * span],
                ],
                axis=0,
            )
            gate = jnp.dot(x, wg_ref[...], preferred_element_type=F32)
            up = jnp.dot(x, wu_ref[...], preferred_element_type=F32)
            low = lax.dot_general(x, left, NT, preferred_element_type=F32)
            if turn == 0:
                right_ref[...] = jnp.zeros_like(right_ref)
            else:
                gate += gate_ref[...]
                up += up_ref[...]
                low += low_ref[...]
            ranks = (half ^ (there >> 1)) * 64 + (there & 1) * 16
            r0 = pl.multiple_of(ranks, 16)
            r1 = pl.multiple_of(ranks + 32, 16)
            right_ref[pl.ds(r0, 16), 0:width] = pack[near + 48 : near + 64, 0:width]
            right_ref[pl.ds(r1, 16), width : 2 * width] = pack[
                near + 48 : near + 64, width : 2 * width
            ]
            cols = outr_ref.shape[2]
            outr_ref[0, turn * 16 : turn * 16 + 16, :] = pack[near + 32 : near + 48, 0:cols]
            outr_ref[1, turn * 16 : turn * 16 + 16, :] = pack[across + 32 : across + 48, 0:cols]
            if turn < 3:
                gate_ref[...], up_ref[...], low_ref[...] = gate, up, low
                return
            scaled = (ADAPTER_SCALE * low).astype(BF16)
            gate += jnp.dot(scaled, right_ref[:, 0:width], preferred_element_type=F32)
            up += jnp.dot(scaled, right_ref[:, width : 2 * width], preferred_element_type=F32)
            hidden = (jax.nn.silu(gate) * up).astype(BF16)
            hidden_ref[...] = hidden
            left = jnp.concatenate(
                [
                    packs[t % 2][
                        ROWS_AT[t // 2][0] + 48 : ROWS_AT[t // 2][0] + 64, 2 * width : 3 * width
                    ]
                    for t in range(4)
                ],
                axis=0,
            )
            mid = lax.dot_general(hidden, left, NT, preferred_element_type=F32)
            mid_ref[...] = (ADAPTER_SCALE * mid).astype(BF16)

    @pl.when(step >= 4)
    def _():
        cols = out_ref.shape[1]
        start = (step - 4) * cols
        side = start // outr_ref.shape[2]
        offset = pl.multiple_of(start - side * outr_ref.shape[2], cols)
        out = jnp.dot(hidden_ref[...], wd_ref[...], preferred_element_type=F32)
        out += jnp.dot(
            mid_ref[...], outr_ref[half ^ side, :, pl.ds(offset, cols)], preferred_element_type=F32
        )
        out_ref[...] = out.astype(BF16)


def feed_forward(place, x, wg, wu, wd, own, far, limit):
    rows, width = x.shape
    hidden = wg.shape[1]
    span, cols = width // 4, 1024
    turn = lambda i, s: s[0] ^ jnp.minimum(i, 3)
    later = lambda i: jnp.maximum(i - 4, 0)
    whole = lambda a: pl.BlockSpec(a.shape, lambda i, s: (0,) * a.ndim)
    return pl.pallas_call(
        ffn_body,
        grid_spec=pltpu.PrefetchScalarGridSpec(
            num_scalar_prefetch=1,
            grid=(4 + width // cols,),
            in_specs=[
                pl.BlockSpec((rows, span), lambda i, s: (0, turn(i, s))),
                pl.BlockSpec((span, hidden), lambda i, s: (turn(i, s), 0)),
                pl.BlockSpec((span, hidden), lambda i, s: (turn(i, s), 0)),
                pl.BlockSpec((hidden, cols), lambda i, s: (0, later(i))),
                whole(own),
                whole(far),
            ],
            out_specs=pl.BlockSpec((rows, cols), lambda i, s: (0, later(i))),
            scratch_shapes=[
                pltpu.VMEM((rows, hidden), F32),
                pltpu.VMEM((rows, hidden), F32),
                pltpu.VMEM((rows, 128), F32),
                pltpu.VMEM((128, 2 * hidden), BF16),
                pltpu.VMEM((rows, hidden), BF16),
                pltpu.VMEM((rows, 64), BF16),
                pltpu.VMEM((2, 64, width // 2), BF16),
            ],
        ),
        out_shape=pltpu.HBM((rows, width), BF16),
        compiler_params=pltpu.CompilerParams(vmem_limit_bytes=limit),
        cost_estimate=pl.CostEstimate(
            flops=6 * rows * width * hidden, bytes_accessed=28 << 20, transcendentals=rows * hidden
        ),
        name="feed_forward",
    )(place, x, wg, wu, wd, own, far)


def combine_body(mix_ref, part_ref, *refs):
    out_ref = refs[-1]
    rows = out_ref.shape[0]
    both = jnp.dot(mix_ref[...], part_ref[...], preferred_element_type=F32)
    total = both[0:rows] + both[rows : 2 * rows]
    if len(refs) == 2:
        total += refs[0][...]
    out_ref[...] = total.astype(out_ref.dtype)


def combine(mix, part, base, out_type):
    slots, width = part.shape
    rows = mix.shape[0] // 2
    cols = 1024
    sheet = pl.BlockSpec((rows, cols), lambda i: (0, i))
    in_specs = [
        pl.BlockSpec(mix.shape, lambda i: (0, 0)),
        pl.BlockSpec((slots, cols), lambda i: (0, i)),
    ]
    operands = (mix, part)
    if base is not None:
        in_specs.append(sheet)
        operands += (base,)
    return pl.pallas_call(
        combine_body,
        grid=(width // cols,),
        out_shape=jax.ShapeDtypeStruct((rows, width), out_type),
        in_specs=in_specs,
        out_specs=sheet,
        compiler_params=pltpu.CompilerParams(vmem_limit_bytes=24 << 20),
        cost_estimate=pl.CostEstimate(
            flops=4 * slots * rows * width, bytes_accessed=3 << 20, transcendentals=0
        ),
        name="combine",
    )(*operands)


def gather_factors(input_left, input_right, output_left, output_right):
    left = jnp.transpose(input_left, (2, 0, 1)).reshape(input_left.shape[2], -1)
    right = jnp.concatenate([input_right[0], input_right[1], output_left.T], axis=1)
    wide = right.shape[1]
    pad = lambda a: jnp.pad(a, ((0, 0), (0, wide - a.shape[1])))
    mine = jnp.concatenate([pad(left), pad(output_right), right], axis=0)
    shared = left.shape[0] + output_right.shape[0]
    groups, tensor = lax.axis_size("group"), lax.axis_size("tensor")
    both = [
        (g * tensor + t, (g ^ 2) * tensor + (t ^ 1)) for g in range(groups) for t in range(tensor)
    ]
    across_x = exchange(mine, "group", 2)
    partner = exchange(mine[:shared], "tensor", 1)
    corner = lax.ppermute(mine[:shared], ("group", "tensor"), both)
    return mine, across_x, partner, corner


def on_device(
    tokens,
    expert_norm_gain,
    routing,
    chosen_expert_weights,
    resident_gate_weight,
    resident_up_weight,
    resident_down_weight,
    adapter_input_left,
    adapter_input_right,
    adapter_output_left,
    adapter_output_right,
):
    rows, width = tokens.shape
    position = lax.axis_index("tensor")
    place = jnp.stack([lax.axis_index("group"), position % 2]).astype(jnp.int32)
    pieces = gather_factors(
        adapter_input_left, adapter_input_right, adapter_output_left, adapter_output_right
    )
    route_t, gain = routing.T, expert_norm_gain.reshape(1, width)
    sent = [dispatch(tokens, gain, route_t, first) for first in range(0, CAP, PART)]
    mix = mixing(route_t, chosen_expert_weights.T, rows)

    def travel(value):
        value = value.reshape(2 * EXPERTS, PART, width)
        return lax.all_to_all(value, "tensor", 0, 0, tiled=True).reshape(-1, width)

    weights = (resident_gate_weight, resident_up_weight, resident_down_weight)
    arrived = [travel(value) for value in sent]
    *pieces, arrived[0] = lax.optimization_barrier((*pieces, arrived[0]))
    own = jnp.concatenate(pieces, axis=0)
    far = exchange(own, "group", 1)
    parts = [
        travel(feed_forward(place, x, *weights, own, far, limit))
        for x, limit in zip(arrived, FFN_VMEM)
    ]
    base = combine(mix[0], parts[0], None, F32)
    return combine(mix[1], parts[1], base, BF16)


def solution(mesh):
    return jax.shard_map(
        on_device,
        mesh=mesh,
        in_specs=(
            P(("group", "tensor"), None),
            P(),
            P("group", None),
            P("group", None),
            P(None, "tensor"),
            P(None, "tensor"),
            P("tensor", None),
            P(None, "group", "tensor"),
            P(None, "group", "tensor"),
            P("tensor", "group"),
            P("group", "tensor"),
        ),
        out_specs=P(("group", "tensor"), None),
        check_vma=False,
    )
```

time: 151 us -> 148 us (0.980)
  waiting for transfers between devices: 72.7 us -> 65 us
  Pallas kernels: 42.1 us -> 44 us
    all_to_all x4, waiting for transfers between devices: 67.1 us -> 56.2 us  [travel(): return lax.all_to_all(value, 'tensor', 0, 0, tiled=True).reshape(-1, width)]
    ppermute x1, waiting for transfers between devices: 3.07 us -> 6.31 us  [gather_factors(): corner = lax.ppermute(mine[:shared], ('group', 'tensor'), both)]
    pallas_call x5 -> x7, Pallas kernels: 42.1 us -> 44 us  [the longest x2 30.6 us: feed_forward(): pl.pallas_call(ffn_body, grid_spec=pltpu.PrefetchScalarGridSpec(num_scala...]
    unnamed x21 -> x17, local copies, waits for them, and re-layouts: 3.36 us -> 2.94 us
  transfers between devices with their start and end apart: 8 -> 8, of which waited for: 6 -> 6; matrix products, arithmetic and copies ran while one was open for 1% -> 4% of each run, Pallas kernels for 22% -> 26%
where the time goes in v3:
time: 148 us; the launch traced here: 147 us
  waiting for transfers between devices  65 us (44%)
  Pallas kernels  44 us (30%)
  starting transfers between devices  31.1 us (21%)
  local copies, waits for them, and re-layouts  4.71 us (3%)
  other arithmetic  1.54 us (1%)
    all_to_all x4, waiting for transfers between devices, travel(): return lax.all_to_all(value, 'tensor', 0, 0, tiled=True).reshape(-1, width)  56.2 us
    pallas_call x2, Pallas kernels, feed_forward(): pl.pallas_call(ffn_body, grid_spec=pltpu.PrefetchScalarGridSpec(num_scala...  30.6 us
    all_to_all x4, starting transfers between devices, travel(): return lax.all_to_all(value, 'tensor', 0, 0, tiled=True).reshape(-1, width)  26 us
    pallas_call x2, Pallas kernels, dispatch(): pl.pallas_call(functools.partial(dispatch_body, first), grid=(steps,), ou...  6.86 us
    ppermute x1, waiting for transfers between devices, gather_factors(): corner = lax.ppermute(mine[:shared], ('group', 'tensor'), both)  6.31 us
    pallas_call x2, Pallas kernels, combine(): pl.pallas_call(combine_body, grid=(width // cols,), out_shape=jax.ShapeDt...  4.84 us
  transfers between devices with their start and end apart: 8, of which 6 were waited for; matrix products, arithmetic and copies ran while one was open for 4% of the time, Pallas kernels for 26%

profile of v3, /device:TPU:10, one launch (start us, length us, event | category | flops | bytes accessed | tf_op | source)
XLA Modules:
  0.0 146.6 jit_solution(17280689688765133983)
XLA Ops:
  0.0 3.4 %dispatch.3 = bf16[16,2,8,4096]{3,2,1,0:T(8,128)(2,1)} custom-call(bf16[32,4096]{1,0:T(8,128)(2,1)} %tokens_ref.3, f32[1,4096]{1,0:T(1,128)} %bitcast.35, s32[4,1024]{1,0:T(4,128)} %bitcast.31), custom_call_target="tpu_custom_call" | custom-call | flops 33554432 | bytes 3145728 | tf_op jit(solution)/shard_map/dispatch/pallas_call | solution.py:75
  3.4 9.7 %all-to-all-start.1 = ((bf16[32,8,4096]{2,1,0:T(8,128)(2,1)}), bf16[32,8,4096]{2,1,0:T(8,128)(2,1)}, u32[]{:S(2)}, u32[]{:S(2)}) async-start(bf16[32,8,4096]{2,1,0:T(8,128)(2,1)} %bitcast.27), calls=%async_computation.1 | async-start | bytes 4194304 | tf_op jit(solution)/shard_map/all_to_all | solution.py:318
  14.0 2.1 %collective-permute-start = (bf16[64,2304]{1,0:T(8,128)(2,1)}, bf16[64,2304]{1,0:T(8,128)(2,1)}, u32[]{:S(2)}, u32[]{:S(2)}) collective-permute-start(bf16[64,2304]{1,0:T(8,128)(2,1)} %maximum_maximum_fusion), channel_id=1, source_target_pairs={{0,64},{32,96},{64,0},{96,32},{1,65},{33,97},{65,1},{97,33},{2,66}... | collective-permute-start | bytes 884744 | tf_op jit(solution)/shard_map/ppermute | solution.py:25
  16.8 2.3 %collective-permute-start.2 = (bf16[48,2304]{1,0:T(8,128)(2,1)}, bf16[48,2304]{1,0:T(8,128)(2,1)}, u32[]{:S(2)}, u32[]{:S(2)}) collective-permute-start(bf16[48,2304]{1,0:T(8,128)(2,1)} %pad_maximum_fusion), channel_id=1, source_target_pairs={{0,65},{1,64},{2,67},{3,66},{4,69},{5,68},{6,71},{7,70},{8,73},{9,... | collective-permute-start | bytes 663560 | tf_op jit(solution)/shard_map/ppermute | solution.py:289
  19.7 3.4 %dispatch.2 = bf16[16,2,8,4096]{3,2,1,0:T(8,128)(2,1)} custom-call(bf16[32,4096]{1,0:T(8,128)(2,1)} %tokens_ref.3, f32[1,4096]{1,0:T(1,128)} %bitcast.36, s32[4,1024]{1,0:T(4,128)} %bitcast.32), custom_call_target="tpu_custom_call" | custom-call | flops 33554432 | bytes 3145728 | tf_op jit(solution)/shard_map/dispatch/pallas_call | solution.py:75
  23.1 18.6 %all-to-all-done.1 = bf16[32,8,4096]{2,1,0:T(8,128)(2,1)} async-done(((bf16[32,8,4096]{2,1,0:T(8,128)(2,1)}), bf16[32,8,4096]{2,1,0:T(8,128)(2,1)}, u32[]{:S(2)}, u32[]{:S(2)}) %all-to-all-start.1) | async-done | bytes 2097184 | tf_op jit(solution)/shard_map/all_to_all | solution.py:318
  41.7 5.0 %all-to-all-start = ((bf16[32,8,4096]{2,1,0:T(8,128)(2,1)}), bf16[32,8,4096]{2,1,0:T(8,128)(2,1)}, u32[]{:S(2)}, u32[]{:S(2)}) async-start(bf16[32,8,4096]{2,1,0:T(8,128)(2,1)} %bitcast.26), calls=%async_computation | async-start | bytes 4194304 | tf_op jit(solution)/shard_map/all_to_all | solution.py:318
  46.7 6.3 %collective-permute-done.2 = bf16[48,2304]{1,0:T(8,128)(2,1)} collective-permute-done((bf16[48,2304]{1,0:T(8,128)(2,1)}, bf16[48,2304]{1,0:T(8,128)(2,1)}, u32[]{:S(2)}, u32[]{:S(2)}) %collective-permute-start.2) | collective-permute-done | bytes 221216 | tf_op jit(solution)/shard_map/ppermute | solution.py:289
  53.0 1.0 constant_dynamic-update-slice_fusion.3
  54.0 1.0 constant_dynamic-update-slice_fusion.2
  55.0 1.0 constant_dynamic-update-slice_fusion.1
  55.9 1.0 constant_dynamic-update-slice_fusion.own_ref
  57.1 2.5 %collective-permute-done.3.far_ref = bf16[224,2304]{1,0:T(8,128)(2,1)S(1)} collective-permute-done((bf16[224,2304]{1,0:T(8,128)(2,1)S(1)}, bf16[224,2304]{1,0:T(8,128)(2,1)S(1)}, u32[]{:S(2)}, u32[]{:S(2)}) %collective-permute-start.3) | collective-permute-done | bytes 1032224 | tf_op jit(solution)/shard_map/ppermute | solution.py:25
  59.6 14.8 %feed_forward.3 = bf16[256,4096]{1,0:T(8,128)(2,1)} custom-call(s32[2]{0:T(128)S(1)} %pad_add_fusion.place_ref, bf16[256,4096]{1,0:T(8,128)(2,1)} %bitcast.13.x_ref, bf16[4096,768]{1,0:T(8,128)(2,1)} %wg_ref.3, bf16[4096,768]{1,0:T(8,128)(2,1)} %wu_ref.3, bf16[768,4096]{1,0:T(8,128)(2,1)} %wd_ref.3, ...), custom_call_target="tpu_custom_call" | custom-call | flops 4831838208 | bytes 29360128 | tf_op jit(solution)/shard_map/feed_forward/pallas_call | solution.py:206
  74.4 1.0 all-to-all-done
  75.4 6.6 %all-to-all-start.3 = ((bf16[32,8,4096]{2,1,0:T(8,128)(2,1)}), bf16[32,8,4096]{2,1,0:T(8,128)(2,1)}, u32[]{:S(2)}, u32[]{:S(2)}) async-start(bf16[32,8,4096]{2,1,0:T(8,128)(2,1)} %bitcast.29), calls=%async_computation.3 | async-start | bytes 4194304 | tf_op jit(solution)/shard_map/all_to_all | solution.py:318
  82.1 15.9 %feed_forward.2 = bf16[256,4096]{1,0:T(8,128)(2,1)} custom-call(s32[2]{0:T(128)} %copy-done.2, bf16[256,4096]{1,0:T(8,128)(2,1)} %bitcast.7.x_ref, bf16[4096,768]{1,0:T(8,128)(2,1)} %wg_ref.3, bf16[4096,768]{1,0:T(8,128)(2,1)} %wu_ref.3, bf16[768,4096]{1,0:T(8,128)(2,1)} %wd_ref.3, bf16[224,2304]{1,0:T(8,128)(2,1)} %copy-done, bf16[224,2304]{1,0:T(8,128)(2,1)} %copy-done.1), custom_call_target="tpu_custom_call" | custom-call | flops 4831838208 | bytes 29360128 | tf_op jit(solution)/shard_map/feed_forward/pallas_call | solution.py:206
  97.9 13.3 %all-to-all-done.3 = bf16[32,8,4096]{2,1,0:T(8,128)(2,1)} async-done(((bf16[32,8,4096]{2,1,0:T(8,128)(2,1)}), bf16[32,8,4096]{2,1,0:T(8,128)(2,1)}, u32[]{:S(2)}, u32[]{:S(2)}) %all-to-all-start.3) | async-done | bytes 2097184 | tf_op jit(solution)/shard_map/all_to_all | solution.py:318
  111.2 4.7 %all-to-all-start.2 = ((bf16[32,8,4096]{2,1,0:T(8,128)(2,1)}), bf16[32,8,4096]{2,1,0:T(8,128)(2,1)S(1)}, u32[]{:S(2)}, u32[]{:S(2)}) async-start(bf16[32,8,4096]{2,1,0:T(8,128)(2,1)} %bitcast.28), calls=%async_computation.2 | async-start | bytes 4194304 | tf_op jit(solution)/shard_map/all_to_all | solution.py:318
  116.0 1.7 %mixing.1 = bf16[2,64,256]{2,1,0:T(8,128)(2,1)} custom-call(s32[4,1024]{1,0:T(4,128)} %bitcast.33, f32[4,1024]{1,0:T(4,128)} %bitcast.38), custom_call_target="tpu_custom_call" | custom-call | flops 1048576 | bytes 131072 | tf_op jit(solution)/shard_map/mixing/pallas_call | solution.py:110
  117.6 0.8 slice_bitcast_fusion
  118.4 2.8 %combine.2.refs_0_ = f32[32,4096]{1,0:T(8,128)S(1)} custom-call(bf16[64,256]{1,0:T(8,128)(2,1)S(1)} %get-tuple-element.15.mix_ref, bf16[256,4096]{1,0:T(8,128)(2,1)} %bitcast.18.part_ref), custom_call_target="tpu_custom_call" | custom-call | flops 134217728 | bytes 3145728 | tf_op jit(solution)/shard_map/combine/pallas_call | solution.py:262
  121.2 23.3 %all-to-all-done.2 = bf16[32,8,4096]{2,1,0:T(8,128)(2,1)S(1)} async-done(((bf16[32,8,4096]{2,1,0:T(8,128)(2,1)}), bf16[32,8,4096]{2,1,0:T(8,128)(2,1)S(1)}, u32[]{:S(2)}, u32[]{:S(2)}) %all-to-all-start.2) | async-done | bytes 2097184 | tf_op jit(solution)/shard_map/all_to_all | solution.py:318
  144.5 2.1 %combine.3 = bf16[32,4096]{1,0:T(8,128)(2,1)} custom-call(bf16[64,256]{1,0:T(8,128)(2,1)S(1)} %get-tuple-element.16.mix_ref, bf16[256,4096]{1,0:T(8,128)(2,1)S(1)} %bitcast.25, f32[32,4096]{1,0:T(8,128)S(1)} %combine.2.refs_0_), custom_call_target="tpu_custom_call" | custom-call | flops 134217728 | bytes 3145728 | tf_op jit(solution)/shard_map/combine/pallas_call | solution.py:262
  (25 shorter events, 2.2 us)
Async XLA Ops:
  3.4 9.7 %copy-start.3 = (bf16[2,1024,32]{1,2,0:T(8,128)(2,1)S(1)}, bf16[2,1024,32]{1,2,0:T(8,128)(2,1)}, u32[]{:S(2)}) copy-start(bf16[2,1024,32]{1,2,0:T(8,128)(2,1)} %param.18) | copy-start | bytes 393220
  3.4 9.7 %copy-start.4 = (bf16[16,2048]{1,0:T(8,128)(2,1)S(1)}, bf16[16,2048]{1,0:T(8,128)(2,1)}, u32[]{:S(2)}) copy-start(bf16[16,2048]{1,0:T(8,128)(2,1)} %param.21) | copy-start | bytes 196612
  3.4 9.8 %copy-start.5 = (bf16[2,16,768]{2,1,0:T(8,128)(2,1)S(1)}, bf16[2,16,768]{2,1,0:T(8,128)(2,1)}, u32[]{:S(2)}) copy-start(bf16[2,16,768]{2,1,0:T(8,128)(2,1)} %param.19) | copy-start | bytes 147460
  3.4 9.8 %copy-start.6 = (bf16[768,16]{0,1:T(8,128)(2,1)S(1)}, bf16[768,16]{0,1:T(8,128)(2,1)}, u32[]{:S(2)}) copy-start(bf16[768,16]{0,1:T(8,128)(2,1)} %param.20) | copy-start | bytes 73732
  3.4 38.3 %all-to-all-start.1 = ((bf16[32,8,4096]{2,1,0:T(8,128)(2,1)}), bf16[32,8,4096]{2,1,0:T(8,128)(2,1)}, u32[]{:S(2)}, u32[]{:S(2)}) async-start(bf16[32,8,4096]{2,1,0:T(8,128)(2,1)} %bitcast.27), calls=%async_computation.1 | async-start | bytes 4194304 | tf_op jit(solution)/shard_map/all_to_all | solution.py:318
  14.0 39.0 %collective-permute-start = (bf16[64,2304]{1,0:T(8,128)(2,1)}, bf16[64,2304]{1,0:T(8,128)(2,1)}, u32[]{:S(2)}, u32[]{:S(2)}) collective-permute-start(bf16[64,2304]{1,0:T(8,128)(2,1)} %maximum_maximum_fusion), channel_id=1, source_target_pairs={{0,64},{32,96},{64,0},{96,32},{1,65},{33,97},{65,1},{97,33},{2,66}... | collective-permute-start | bytes 884744 | tf_op jit(solution)/shard_map/ppermute | solution.py:25
  16.8 36.2 %collective-permute-start.2 = (bf16[48,2304]{1,0:T(8,128)(2,1)}, bf16[48,2304]{1,0:T(8,128)(2,1)}, u32[]{:S(2)}, u32[]{:S(2)}) collective-permute-start(bf16[48,2304]{1,0:T(8,128)(2,1)} %pad_maximum_fusion), channel_id=1, source_target_pairs={{0,65},{1,64},{2,67},{3,66},{4,69},{5,68},{6,71},{7,70},{8,73},{9,... | collective-permute-start | bytes 663560 | tf_op jit(solution)/shard_map/ppermute | solution.py:289
  19.1 33.9 %collective-permute-start.1 = (bf16[48,2304]{1,0:T(8,128)(2,1)}, bf16[48,2304]{1,0:T(8,128)(2,1)}, u32[]{:S(2)}, u32[]{:S(2)}) collective-permute-start(bf16[48,2304]{1,0:T(8,128)(2,1)} %pad_maximum_fusion), channel_id=1, source_target_pairs={{0,1},{1,0},{2,3},{3,2},{4,5},{5,4},{6,7},{7,6},{8,9},{9,8},{10,11... | collective-permute-start | bytes 663560 | tf_op jit(solution)/shard_map/ppermute | solution.py:25
  41.7 33.7 %all-to-all-start = ((bf16[32,8,4096]{2,1,0:T(8,128)(2,1)}), bf16[32,8,4096]{2,1,0:T(8,128)(2,1)}, u32[]{:S(2)}, u32[]{:S(2)}) async-start(bf16[32,8,4096]{2,1,0:T(8,128)(2,1)} %bitcast.26), calls=%async_computation | async-start | bytes 4194304 | tf_op jit(solution)/shard_map/all_to_all | solution.py:318
  56.9 17.5 %copy-start = (bf16[224,2304]{1,0:T(8,128)(2,1)}, bf16[224,2304]{1,0:T(8,128)(2,1)S(1)}, u32[]{:S(2)}) copy-start(bf16[224,2304]{1,0:T(8,128)(2,1)S(1)} %constant_dynamic-update-slice_fusion.own_ref) | copy-start | bytes 3096580
  56.9 2.7 %collective-permute-start.3 = (bf16[224,2304]{1,0:T(8,128)(2,1)S(1)}, bf16[224,2304]{1,0:T(8,128)(2,1)S(1)}, u32[]{:S(2)}, u32[]{:S(2)}) collective-permute-start(bf16[224,2304]{1,0:T(8,128)(2,1)S(1)} %constant_dynamic-update-slice_fusion.own_ref), channel_id=1, source_target_pairs={{0,32},{32,0},{64,96},{96,64},{1,33},{33,1},{65,97},{97,65},{2,34}... | collective-permute-start | bytes 3096584 | tf_op jit(solution)/shard_map/ppermute | solution.py:25
  57.1 17.3 %copy-start.2 = (s32[2]{0:T(128)}, s32[2]{0:T(128)S(1)}, u32[]{:S(2)}) copy-start(s32[2]{0:T(128)S(1)} %pad_add_fusion.place_ref) | copy-start | bytes 28
  59.6 14.8 %copy-start.1 = (bf16[224,2304]{1,0:T(8,128)(2,1)}, bf16[224,2304]{1,0:T(8,128)(2,1)S(1)}, u32[]{:S(2)}) copy-start(bf16[224,2304]{1,0:T(8,128)(2,1)S(1)} %collective-permute-done.3.far_ref) | copy-start | bytes 3096580
  75.4 35.8 %all-to-all-start.3 = ((bf16[32,8,4096]{2,1,0:T(8,128)(2,1)}), bf16[32,8,4096]{2,1,0:T(8,128)(2,1)}, u32[]{:S(2)}, u32[]{:S(2)}) async-start(bf16[32,8,4096]{2,1,0:T(8,128)(2,1)} %bitcast.29), calls=%async_computation.3 | async-start | bytes 4194304 | tf_op jit(solution)/shard_map/all_to_all | solution.py:318
  111.2 33.3 %all-to-all-start.2 = ((bf16[32,8,4096]{2,1,0:T(8,128)(2,1)}), bf16[32,8,4096]{2,1,0:T(8,128)(2,1)S(1)}, u32[]{:S(2)}, u32[]{:S(2)}) async-start(bf16[32,8,4096]{2,1,0:T(8,128)(2,1)} %bitcast.28), calls=%async_computation.2 | async-start | bytes 4194304 | tf_op jit(solution)/shard_map/all_to_all | solution.py:318

commit v4 on v3

--- a/solution.py
+++ b/solution.py
@@ -70,7 +70,7 @@
 
 def dispatch(tokens, gain, route_t, first):
     rows, width = tokens.shape
-    steps = 4
+    steps = 2
     per = EXPERTS // steps
     return pl.pallas_call(
         functools.partial(dispatch_body, first),
@@ -249,7 +249,7 @@
 def combine(mix, part, base, out_type):
     slots, width = part.shape
     rows = mix.shape[0] // 2
-    cols = 1024
+    cols = width
     sheet = pl.BlockSpec((rows, cols), lambda i: (0, i))
     in_specs = [
         pl.BlockSpec(mix.shape, lambda i: (0, 0)),
@@ -265,12 +265,22 @@
         out_shape=jax.ShapeDtypeStruct((rows, width), out_type),
         in_specs=in_specs,
         out_specs=sheet,
-        compiler_params=pltpu.CompilerParams(vmem_limit_bytes=24 << 20),
+        compiler_params=pltpu.CompilerParams(vmem_limit_bytes=32 << 20),
         cost_estimate=pl.CostEstimate(
             flops=4 * slots * rows * width, bytes_accessed=3 << 20, transcendentals=0
         ),
         name="combine",
     )(*operands)
+
+
+def stack(pieces):
+    rows, total, at = sum(piece.shape[0] for piece in pieces), None, 0
+    for piece in pieces:
+        after = rows - at - piece.shape[0]
+        padded = jnp.pad(piece, ((at, after), (0, 0)))
+        total = padded if total is None else total + padded
+        at += piece.shape[0]
+    return total
 
 
 def gather_factors(input_left, input_right, output_left, output_right):
@@ -320,7 +330,7 @@
     weights = (resident_gate_weight, resident_up_weight, resident_down_weight)
     arrived = [travel(value) for value in sent]
     *pieces, arrived[0] = lax.optimization_barrier((*pieces, arrived[0]))
-    own = jnp.concatenate(pieces, axis=0)
+    own = stack(pieces)
     far = exchange(own, "group", 1)
     parts = [
         travel(feed_forward(place, x, *weights, own, far, limit))

time: 148 us -> 146 us (0.986)
  waiting for transfers between devices: 65 us -> 69.1 us
  local copies, waits for them, and re-layouts: 4.71 us -> 0.84 us
  Pallas kernels: 44 us -> 41.2 us
    all_to_all x4, waiting for transfers between devices: 56.2 us -> 60.2 us  [travel(): return lax.all_to_all(value, 'tensor', 0, 0, tiled=True).reshape(-1, width)]
    unnamed x17 -> x14, local copies, waits for them, and re-layouts: 2.94 us -> 0.03 us
    pallas_call x2, Pallas kernels: 4.84 us -> 3.24 us  [combine(): pl.pallas_call(combine_body, grid=(width // cols,), out_shape=jax.ShapeDt...]
  transfers between devices with their start and end apart: 8 -> 8, of which waited for: 6 -> 6; matrix products, arithmetic and copies ran while one was open for 4% -> 3% of each run, Pallas kernels for 26% -> 26%
where the time goes in v4:
time: 146 us; the launch traced here: 145 us
  waiting for transfers between devices  69.1 us (47%)
  Pallas kernels  41.2 us (28%)
  starting transfers between devices  30.9 us (21%)
  other arithmetic  2.88 us (2%)
    all_to_all x4, waiting for transfers between devices, travel(): return lax.all_to_all(value, 'tensor', 0, 0, tiled=True).reshape(-1, width)  60.2 us
    pallas_call x2, Pallas kernels, feed_forward(): pl.pallas_call(ffn_body, grid_spec=pltpu.PrefetchScalarGridSpec(num_scala...  30.6 us
    all_to_all x4, starting transfers between devices, travel(): return lax.all_to_all(value, 'tensor', 0, 0, tiled=True).reshape(-1, width)  25.8 us
    ppermute x1, waiting for transfers between devices, gather_factors(): corner = lax.ppermute(mine[:shared], ('group', 'tensor'), both)  6.32 us
    pallas_call x2, Pallas kernels, dispatch(): pl.pallas_call(functools.partial(dispatch_body, first), grid=(steps,), ou...  5.6 us
    pallas_call x2, Pallas kernels, combine(): pl.pallas_call(combine_body, grid=(width // cols,), out_shape=jax.ShapeDt...  3.24 us
  transfers between devices with their start and end apart: 8, of which 6 were waited for; matrix products, arithmetic and copies ran while one was open for 3% of the time, Pallas kernels for 26%

profile of v4, /device:TPU:10, one launch (start us, length us, event | category | flops | bytes accessed | tf_op | source)
XLA Modules:
  0.0 145.0 jit_solution(10871749752304430536)
XLA Ops:
  0.0 2.8 %dispatch.3 = bf16[16,2,8,4096]{3,2,1,0:T(8,128)(2,1)} custom-call(bf16[32,4096]{1,0:T(8,128)(2,1)} %tokens_ref.3, f32[1,4096]{1,0:T(1,128)} %bitcast.35, s32[4,1024]{1,0:T(4,128)} %bitcast.31), custom_call_target="tpu_custom_call" | custom-call | flops 33554432 | bytes 3145728 | tf_op jit(solution)/shard_map/dispatch/pallas_call | solution.py:75
  2.8 9.7 %all-to-all-start.1 = ((bf16[32,8,4096]{2,1,0:T(8,128)(2,1)}), bf16[32,8,4096]{2,1,0:T(8,128)(2,1)}, u32[]{:S(2)}, u32[]{:S(2)}) async-start(bf16[32,8,4096]{2,1,0:T(8,128)(2,1)} %bitcast.27), calls=%async_computation.1 | async-start | bytes 4194304 | tf_op jit(solution)/shard_map/all_to_all | solution.py:328
  12.6 0.8 maximum_maximum_fusion
  13.3 2.1 %collective-permute-start = (bf16[64,2304]{1,0:T(8,128)(2,1)}, bf16[64,2304]{1,0:T(8,128)(2,1)}, u32[]{:S(2)}, u32[]{:S(2)}) collective-permute-start(bf16[64,2304]{1,0:T(8,128)(2,1)} %maximum_maximum_fusion), channel_id=1, source_target_pairs={{0,64},{32,96},{64,0},{96,32},{1,65},{33,97},{65,1},{97,33},{2,66}... | collective-permute-start | bytes 884744 | tf_op jit(solution)/shard_map/ppermute | solution.py:25
  15.5 0.7 pad_maximum_fusion
  16.2 2.3 %collective-permute-start.2 = (bf16[48,2304]{1,0:T(8,128)(2,1)}, bf16[48,2304]{1,0:T(8,128)(2,1)}, u32[]{:S(2)}, u32[]{:S(2)}) collective-permute-start(bf16[48,2304]{1,0:T(8,128)(2,1)} %pad_maximum_fusion), channel_id=1, source_target_pairs={{0,65},{1,64},{2,67},{3,66},{4,69},{5,68},{6,71},{7,70},{8,73},{9,... | collective-permute-start | bytes 663560 | tf_op jit(solution)/shard_map/ppermute | solution.py:299
  18.5 0.6 collective-permute-start.1
  19.0 2.8 %dispatch.2 = bf16[16,2,8,4096]{3,2,1,0:T(8,128)(2,1)} custom-call(bf16[32,4096]{1,0:T(8,128)(2,1)} %tokens_ref.3, f32[1,4096]{1,0:T(1,128)} %bitcast.36, s32[4,1024]{1,0:T(4,128)} %bitcast.32), custom_call_target="tpu_custom_call" | custom-call | flops 33554432 | bytes 3145728 | tf_op jit(solution)/shard_map/dispatch/pallas_call | solution.py:75
  21.8 19.2 %all-to-all-done.1 = bf16[32,8,4096]{2,1,0:T(8,128)(2,1)} async-done(((bf16[32,8,4096]{2,1,0:T(8,128)(2,1)}), bf16[32,8,4096]{2,1,0:T(8,128)(2,1)}, u32[]{:S(2)}, u32[]{:S(2)}) %all-to-all-start.1) | async-done | bytes 2097184 | tf_op jit(solution)/shard_map/all_to_all | solution.py:328
  41.1 5.0 %all-to-all-start = ((bf16[32,8,4096]{2,1,0:T(8,128)(2,1)}), bf16[32,8,4096]{2,1,0:T(8,128)(2,1)}, u32[]{:S(2)}, u32[]{:S(2)}) async-start(bf16[32,8,4096]{2,1,0:T(8,128)(2,1)} %bitcast.26), calls=%async_computation | async-start | bytes 4194304 | tf_op jit(solution)/shard_map/all_to_all | solution.py:328
  46.1 6.3 %collective-permute-done.2 = bf16[48,2304]{1,0:T(8,128)(2,1)} collective-permute-done((bf16[48,2304]{1,0:T(8,128)(2,1)}, bf16[48,2304]{1,0:T(8,128)(2,1)}, u32[]{:S(2)}, u32[]{:S(2)}) %collective-permute-start.2) | collective-permute-done | bytes 221216 | tf_op jit(solution)/shard_map/ppermute | solution.py:299
  52.4 1.3 pad_add_fusion.own_ref
  53.9 2.5 %collective-permute-done.3.far_ref = bf16[224,2304]{1,0:T(8,128)(2,1)S(1)} collective-permute-done((bf16[224,2304]{1,0:T(8,128)(2,1)S(1)}, bf16[224,2304]{1,0:T(8,128)(2,1)S(1)}, u32[]{:S(2)}, u32[]{:S(2)}) %collective-permute-start.3) | collective-permute-done | bytes 1032224 | tf_op jit(solution)/shard_map/ppermute | solution.py:25
  56.5 14.8 %feed_forward.3 = bf16[256,4096]{1,0:T(8,128)(2,1)} custom-call(s32[2]{0:T(128)S(1)} %pad_add_fusion.1.place_ref, bf16[256,4096]{1,0:T(8,128)(2,1)} %bitcast.13.x_ref, bf16[4096,768]{1,0:T(8,128)(2,1)} %wg_ref.3, bf16[4096,768]{1,0:T(8,128)(2,1)} %wu_ref.3, bf16[768,4096]{1,0:T(8,128)(2,1)} %wd_ref.3, bf16[224,2304]{1,0:T(8,128)(2,1)S(1)} %pad_add_fusion.own_ref, ...), custom_call_target="tpu_custom_call" | custom-call | flops 4831838208 | bytes 29360128 | tf_op jit(solution)/shard_map/feed_forward/pallas_call | solution.py:206
  71.2 3.5 %all-to-all-done = bf16[32,8,4096]{2,1,0:T(8,128)(2,1)} async-done(((bf16[32,8,4096]{2,1,0:T(8,128)(2,1)}), bf16[32,8,4096]{2,1,0:T(8,128)(2,1)}, u32[]{:S(2)}, u32[]{:S(2)}) %all-to-all-start) | async-done | bytes 2097184 | tf_op jit(solution)/shard_map/all_to_all | solution.py:328
  74.7 6.4 %all-to-all-start.3 = ((bf16[32,8,4096]{2,1,0:T(8,128)(2,1)}), bf16[32,8,4096]{2,1,0:T(8,128)(2,1)}, u32[]{:S(2)}, u32[]{:S(2)}) async-start(bf16[32,8,4096]{2,1,0:T(8,128)(2,1)} %bitcast.29), calls=%async_computation.3 | async-start | bytes 4194304 | tf_op jit(solution)/shard_map/all_to_all | solution.py:328
  81.2 15.9 %feed_forward.2 = bf16[256,4096]{1,0:T(8,128)(2,1)} custom-call(s32[2]{0:T(128)} %copy-done.2, bf16[256,4096]{1,0:T(8,128)(2,1)} %bitcast.7.x_ref, bf16[4096,768]{1,0:T(8,128)(2,1)} %wg_ref.3, bf16[4096,768]{1,0:T(8,128)(2,1)} %wu_ref.3, bf16[768,4096]{1,0:T(8,128)(2,1)} %wd_ref.3, bf16[224,2304]{1,0:T(8,128)(2,1)} %copy-done, bf16[224,2304]{1,0:T(8,128)(2,1)} %copy-done.1), custom_call_target="tpu_custom_call" | custom-call | flops 4831838208 | bytes 29360128 | tf_op jit(solution)/shard_map/feed_forward/pallas_call | solution.py:206
  97.0 13.1 %all-to-all-done.3 = bf16[32,8,4096]{2,1,0:T(8,128)(2,1)} async-done(((bf16[32,8,4096]{2,1,0:T(8,128)(2,1)}), bf16[32,8,4096]{2,1,0:T(8,128)(2,1)}, u32[]{:S(2)}, u32[]{:S(2)}) %all-to-all-start.3) | async-done | bytes 2097184 | tf_op jit(solution)/shard_map/all_to_all | solution.py:328
  110.1 4.8 %all-to-all-start.2 = ((bf16[32,8,4096]{2,1,0:T(8,128)(2,1)}), bf16[32,8,4096]{2,1,0:T(8,128)(2,1)S(1)}, u32[]{:S(2)}, u32[]{:S(2)}) async-start(bf16[32,8,4096]{2,1,0:T(8,128)(2,1)} %bitcast.28), calls=%async_computation.2 | async-start | bytes 4194304 | tf_op jit(solution)/shard_map/all_to_all | solution.py:328
  114.9 1.7 %mixing.1 = bf16[2,64,256]{2,1,0:T(8,128)(2,1)} custom-call(s32[4,1024]{1,0:T(4,128)} %bitcast.33, f32[4,1024]{1,0:T(4,128)} %bitcast.38), custom_call_target="tpu_custom_call" | custom-call | flops 1048576 | bytes 131072 | tf_op jit(solution)/shard_map/mixing/pallas_call | solution.py:110
  116.6 0.8 slice_bitcast_fusion
  117.4 2.1 %combine.2.refs_0_ = f32[32,4096]{1,0:T(8,128)S(1)} custom-call(bf16[64,256]{1,0:T(8,128)(2,1)S(1)} %get-tuple-element.15.mix_ref, bf16[256,4096]{1,0:T(8,128)(2,1)} %bitcast.18.part_ref), custom_call_target="tpu_custom_call" | custom-call | flops 134217728 | bytes 3145728 | tf_op jit(solution)/shard_map/combine/pallas_call | solution.py:262
  119.4 24.4 %all-to-all-done.2 = bf16[32,8,4096]{2,1,0:T(8,128)(2,1)S(1)} async-done(((bf16[32,8,4096]{2,1,0:T(8,128)(2,1)}), bf16[32,8,4096]{2,1,0:T(8,128)(2,1)S(1)}, u32[]{:S(2)}, u32[]{:S(2)}) %all-to-all-start.2) | async-done | bytes 2097184 | tf_op jit(solution)/shard_map/all_to_all | solution.py:328
  143.8 1.2 combine.3
  (22 shorter events, 0.2 us)
Async XLA Ops:
  2.8 9.7 %copy-start.3 = (bf16[2,1024,32]{1,2,0:T(8,128)(2,1)S(1)}, bf16[2,1024,32]{1,2,0:T(8,128)(2,1)}, u32[]{:S(2)}) copy-start(bf16[2,1024,32]{1,2,0:T(8,128)(2,1)} %param.18) | copy-start | bytes 393220
  2.8 9.7 %copy-start.4 = (bf16[16,2048]{1,0:T(8,128)(2,1)S(1)}, bf16[16,2048]{1,0:T(8,128)(2,1)}, u32[]{:S(2)}) copy-start(bf16[16,2048]{1,0:T(8,128)(2,1)} %param.21) | copy-start | bytes 196612
  2.8 9.8 %copy-start.5 = (bf16[2,16,768]{2,1,0:T(8,128)(2,1)S(1)}, bf16[2,16,768]{2,1,0:T(8,128)(2,1)}, u32[]{:S(2)}) copy-start(bf16[2,16,768]{2,1,0:T(8,128)(2,1)} %param.19) | copy-start | bytes 147460
  2.8 9.8 %copy-start.6 = (bf16[768,16]{0,1:T(8,128)(2,1)S(1)}, bf16[768,16]{0,1:T(8,128)(2,1)}, u32[]{:S(2)}) copy-start(bf16[768,16]{0,1:T(8,128)(2,1)} %param.20) | copy-start | bytes 73732
  2.8 38.3 %all-to-all-start.1 = ((bf16[32,8,4096]{2,1,0:T(8,128)(2,1)}), bf16[32,8,4096]{2,1,0:T(8,128)(2,1)}, u32[]{:S(2)}, u32[]{:S(2)}) async-start(bf16[32,8,4096]{2,1,0:T(8,128)(2,1)} %bitcast.27), calls=%async_computation.1 | async-start | bytes 4194304 | tf_op jit(solution)/shard_map/all_to_all | solution.py:328
  13.3 39.0 %collective-permute-start = (bf16[64,2304]{1,0:T(8,128)(2,1)}, bf16[64,2304]{1,0:T(8,128)(2,1)}, u32[]{:S(2)}, u32[]{:S(2)}) collective-permute-start(bf16[64,2304]{1,0:T(8,128)(2,1)} %maximum_maximum_fusion), channel_id=1, source_target_pairs={{0,64},{32,96},{64,0},{96,32},{1,65},{33,97},{65,1},{97,33},{2,66}... | collective-permute-start | bytes 884744 | tf_op jit(solution)/shard_map/ppermute | solution.py:25
  16.2 36.2 %collective-permute-start.2 = (bf16[48,2304]{1,0:T(8,128)(2,1)}, bf16[48,2304]{1,0:T(8,128)(2,1)}, u32[]{:S(2)}, u32[]{:S(2)}) collective-permute-start(bf16[48,2304]{1,0:T(8,128)(2,1)} %pad_maximum_fusion), channel_id=1, source_target_pairs={{0,65},{1,64},{2,67},{3,66},{4,69},{5,68},{6,71},{7,70},{8,73},{9,... | collective-permute-start | bytes 663560 | tf_op jit(solution)/shard_map/ppermute | solution.py:299
  18.5 33.9 %collective-permute-start.1 = (bf16[48,2304]{1,0:T(8,128)(2,1)}, bf16[48,2304]{1,0:T(8,128)(2,1)}, u32[]{:S(2)}, u32[]{:S(2)}) collective-permute-start(bf16[48,2304]{1,0:T(8,128)(2,1)} %pad_maximum_fusion), channel_id=1, source_target_pairs={{0,1},{1,0},{2,3},{3,2},{4,5},{5,4},{6,7},{7,6},{8,9},{9,8},{10,11... | collective-permute-start | bytes 663560 | tf_op jit(solution)/shard_map/ppermute | solution.py:25
  41.1 33.7 %all-to-all-start = ((bf16[32,8,4096]{2,1,0:T(8,128)(2,1)}), bf16[32,8,4096]{2,1,0:T(8,128)(2,1)}, u32[]{:S(2)}, u32[]{:S(2)}) async-start(bf16[32,8,4096]{2,1,0:T(8,128)(2,1)} %bitcast.26), calls=%async_computation | async-start | bytes 4194304 | tf_op jit(solution)/shard_map/all_to_all | solution.py:328
  53.7 17.5 %copy-start = (bf16[224,2304]{1,0:T(8,128)(2,1)}, bf16[224,2304]{1,0:T(8,128)(2,1)S(1)}, u32[]{:S(2)}) copy-start(bf16[224,2304]{1,0:T(8,128)(2,1)S(1)} %pad_add_fusion.own_ref) | copy-start | bytes 3096580
  53.7 2.7 %collective-permute-start.3 = (bf16[224,2304]{1,0:T(8,128)(2,1)S(1)}, bf16[224,2304]{1,0:T(8,128)(2,1)S(1)}, u32[]{:S(2)}, u32[]{:S(2)}) collective-permute-start(bf16[224,2304]{1,0:T(8,128)(2,1)S(1)} %pad_add_fusion.own_ref), channel_id=1, source_target_pairs={{0,32},{32,0},{64,96},{96,64},{1,33},{33,1},{65,97},{97,65},{2,34}... | collective-permute-start | bytes 3096584 | tf_op jit(solution)/shard_map/ppermute | solution.py:25
  53.9 17.3 %copy-start.2 = (s32[2]{0:T(128)}, s32[2]{0:T(128)S(1)}, u32[]{:S(2)}) copy-start(s32[2]{0:T(128)S(1)} %pad_add_fusion.1.place_ref) | copy-start | bytes 28
  56.5 14.8 %copy-start.1 = (bf16[224,2304]{1,0:T(8,128)(2,1)}, bf16[224,2304]{1,0:T(8,128)(2,1)S(1)}, u32[]{:S(2)}) copy-start(bf16[224,2304]{1,0:T(8,128)(2,1)S(1)} %collective-permute-done.3.far_ref) | copy-start | bytes 3096580
  74.7 35.4 %all-to-all-start.3 = ((bf16[32,8,4096]{2,1,0:T(8,128)(2,1)}), bf16[32,8,4096]{2,1,0:T(8,128)(2,1)}, u32[]{:S(2)}, u32[]{:S(2)}) async-start(bf16[32,8,4096]{2,1,0:T(8,128)(2,1)} %bitcast.29), calls=%async_computation.3 | async-start | bytes 4194304 | tf_op jit(solution)/shard_map/all_to_all | solution.py:328
  110.1 33.7 %all-to-all-start.2 = ((bf16[32,8,4096]{2,1,0:T(8,128)(2,1)}), bf16[32,8,4096]{2,1,0:T(8,128)(2,1)S(1)}, u32[]{:S(2)}, u32[]{:S(2)}) async-start(bf16[32,8,4096]{2,1,0:T(8,128)(2,1)} %bitcast.28), calls=%async_computation.2 | async-start | bytes 4194304 | tf_op jit(solution)/shard_map/all_to_all | solution.py:328

commit v5 on v4

--- a/solution.py
+++ b/solution.py
@@ -275,9 +275,10 @@
 
 def stack(pieces):
     rows, total, at = sum(piece.shape[0] for piece in pieces), None, 0
+    wide = max(piece.shape[1] for piece in pieces)
     for piece in pieces:
         after = rows - at - piece.shape[0]
-        padded = jnp.pad(piece, ((at, after), (0, 0)))
+        padded = jnp.pad(piece, ((at, after), (0, wide - piece.shape[1])))
         total = padded if total is None else total + padded
         at += piece.shape[0]
     return total
@@ -289,14 +290,14 @@
     wide = right.shape[1]
     pad = lambda a: jnp.pad(a, ((0, 0), (0, wide - a.shape[1])))
     mine = jnp.concatenate([pad(left), pad(output_right), right], axis=0)
-    shared = left.shape[0] + output_right.shape[0]
     groups, tensor = lax.axis_size("group"), lax.axis_size("tensor")
     both = [
         (g * tensor + t, (g ^ 2) * tensor + (t ^ 1)) for g in range(groups) for t in range(tensor)
     ]
     across_x = exchange(mine, "group", 2)
-    partner = exchange(mine[:shared], "tensor", 1)
-    corner = lax.ppermute(mine[:shared], ("group", "tensor"), both)
+    pair = jnp.concatenate([left, output_right], axis=0)
+    partner = exchange(pair, "tensor", 1)
+    corner = lax.ppermute(pair, ("group", "tensor"), both)
     return mine, across_x, partner, corner
 
 

time: 146 us -> 145 us (level)
  no operation moved by 1% of the time
where the time goes in v5:
time: 145 us; the launch traced here: 144 us
  waiting for transfers between devices  68 us (47%)
  Pallas kernels  41.2 us (28%)
  starting transfers between devices  30.7 us (21%)
  other arithmetic  2.16 us (1%)
  local copies, waits for them, and re-layouts  2.12 us (1%)
    all_to_all x4, waiting for transfers between devices, travel(): return lax.all_to_all(value, 'tensor', 0, 0, tiled=True).reshape(-1, width)  60.4 us
    pallas_call x2, Pallas kernels, feed_forward(): pl.pallas_call(ffn_body, grid_spec=pltpu.PrefetchScalarGridSpec(num_scala...  30.6 us
    all_to_all x4, starting transfers between devices, travel(): return lax.all_to_all(value, 'tensor', 0, 0, tiled=True).reshape(-1, width)  25.6 us
    pallas_call x2, Pallas kernels, dispatch(): pl.pallas_call(functools.partial(dispatch_body, first), grid=(steps,), ou...  5.6 us
    ppermute x1, waiting for transfers between devices, gather_factors(): corner = lax.ppermute(pair, ('group', 'tensor'), both)  5.05 us
    pallas_call x2, Pallas kernels, combine(): pl.pallas_call(combine_body, grid=(width // cols,), out_shape=jax.ShapeDt...  3.24 us
  transfers between devices with their start and end apart: 8, of which 6 were waited for; matrix products, arithmetic and copies ran while one was open for 3% of the time, Pallas kernels for 26%

profile of v5, /device:TPU:10, one launch (start us, length us, event | category | flops | bytes accessed | tf_op | source)
XLA Modules:
  0.0 144.3 jit_solution(7822941024401434847)
XLA Ops:
  0.0 2.8 %dispatch.3 = bf16[16,2,8,4096]{3,2,1,0:T(8,128)(2,1)} custom-call(bf16[32,4096]{1,0:T(8,128)(2,1)} %tokens_ref.3, f32[1,4096]{1,0:T(1,128)} %bitcast.36, s32[4,1024]{1,0:T(4,128)} %bitcast.32), custom_call_target="tpu_custom_call" | custom-call | flops 33554432 | bytes 3145728 | tf_op jit(solution)/shard_map/dispatch/pallas_call | solution.py:75
  2.8 9.7 %all-to-all-start.1 = ((bf16[32,8,4096]{2,1,0:T(8,128)(2,1)}), bf16[32,8,4096]{2,1,0:T(8,128)(2,1)}, u32[]{:S(2)}, u32[]{:S(2)}) async-start(bf16[32,8,4096]{2,1,0:T(8,128)(2,1)} %bitcast.27), calls=%async_computation.1 | async-start | bytes 4194304 | tf_op jit(solution)/shard_map/all_to_all | solution.py:329
  12.5 0.8 fusion.4
  13.3 2.1 %collective-permute-start = (bf16[64,2304]{1,0:T(8,128)(2,1)}, bf16[64,2304]{1,0:T(8,128)(2,1)}, u32[]{:S(2)}, u32[]{:S(2)}) collective-permute-start(bf16[64,2304]{1,0:T(8,128)(2,1)} %fusion.4), channel_id=1, source_target_pairs={{0,64},{32,96},{64,0},{96,32},{1,65},{33,97},{65,1},{97,33},{2,66}... | collective-permute-start | bytes 884744 | tf_op jit(solution)/shard_map/ppermute | solution.py:25
  15.4 0.7 constant_dynamic-update-slice_fusion.1
  16.1 0.6 constant_dynamic-update-slice_fusion
  16.7 2.3 %collective-permute-start.2 = (bf16[48,2048]{1,0:T(8,128)(2,1)}, bf16[48,2048]{1,0:T(8,128)(2,1)}, u32[]{:S(2)}, u32[]{:S(2)}) collective-permute-start(bf16[48,2048]{1,0:T(8,128)(2,1)} %constant_dynamic-update-slice_fusion), channel_id=1, source_target_pairs={{0,65},{1,64},{2,67},{3,66},{4,69},{5,68},{6,71},{7,70},{8,73},{9,... | collective-permute-start | bytes 589832 | tf_op jit(solution)/shard_map/ppermute | solution.py:300
  19.6 2.8 %dispatch.2 = bf16[16,2,8,4096]{3,2,1,0:T(8,128)(2,1)} custom-call(bf16[32,4096]{1,0:T(8,128)(2,1)} %tokens_ref.3, f32[1,4096]{1,0:T(1,128)} %bitcast.37, s32[4,1024]{1,0:T(4,128)} %bitcast.33), custom_call_target="tpu_custom_call" | custom-call | flops 33554432 | bytes 3145728 | tf_op jit(solution)/shard_map/dispatch/pallas_call | solution.py:75
  22.4 18.7 %all-to-all-done.1 = bf16[32,8,4096]{2,1,0:T(8,128)(2,1)} async-done(((bf16[32,8,4096]{2,1,0:T(8,128)(2,1)}), bf16[32,8,4096]{2,1,0:T(8,128)(2,1)}, u32[]{:S(2)}, u32[]{:S(2)}) %all-to-all-start.1) | async-done | bytes 2097184 | tf_op jit(solution)/shard_map/all_to_all | solution.py:329
  41.1 5.0 %all-to-all-start = ((bf16[32,8,4096]{2,1,0:T(8,128)(2,1)}), bf16[32,8,4096]{2,1,0:T(8,128)(2,1)}, u32[]{:S(2)}, u32[]{:S(2)}) async-start(bf16[32,8,4096]{2,1,0:T(8,128)(2,1)} %bitcast.26), calls=%async_computation | async-start | bytes 4194304 | tf_op jit(solution)/shard_map/all_to_all | solution.py:329
  46.1 5.1 %collective-permute-done.2 = bf16[48,2048]{1,0:T(8,128)(2,1)} collective-permute-done((bf16[48,2048]{1,0:T(8,128)(2,1)}, bf16[48,2048]{1,0:T(8,128)(2,1)}, u32[]{:S(2)}, u32[]{:S(2)}) %collective-permute-start.2) | collective-permute-done | bytes 196640 | tf_op jit(solution)/shard_map/ppermute | solution.py:300
  51.1 1.3 pad_add_fusion.own_ref
  52.6 2.5 %collective-permute-done.3.far_ref = bf16[224,2304]{1,0:T(8,128)(2,1)S(1)} collective-permute-done((bf16[224,2304]{1,0:T(8,128)(2,1)S(1)}, bf16[224,2304]{1,0:T(8,128)(2,1)S(1)}, u32[]{:S(2)}, u32[]{:S(2)}) %collective-permute-start.3) | collective-permute-done | bytes 1032224 | tf_op jit(solution)/shard_map/ppermute | solution.py:25
  55.2 14.8 %feed_forward.3 = bf16[256,4096]{1,0:T(8,128)(2,1)} custom-call(s32[2]{0:T(128)S(1)} %pad_add_fusion.1.place_ref, bf16[256,4096]{1,0:T(8,128)(2,1)} %bitcast.13.x_ref, bf16[4096,768]{1,0:T(8,128)(2,1)} %wg_ref.3, bf16[4096,768]{1,0:T(8,128)(2,1)} %wu_ref.3, bf16[768,4096]{1,0:T(8,128)(2,1)} %wd_ref.3, bf16[224,2304]{1,0:T(8,128)(2,1)S(1)} %pad_add_fusion.own_ref, ...), custom_call_target="tpu_custom_call" | custom-call | flops 4831838208 | bytes 29360128 | tf_op jit(solution)/shard_map/feed_forward/pallas_call | solution.py:206
  70.0 4.3 %all-to-all-done = bf16[32,8,4096]{2,1,0:T(8,128)(2,1)} async-done(((bf16[32,8,4096]{2,1,0:T(8,128)(2,1)}), bf16[32,8,4096]{2,1,0:T(8,128)(2,1)}, u32[]{:S(2)}, u32[]{:S(2)}) %all-to-all-start) | async-done | bytes 2097184 | tf_op jit(solution)/shard_map/all_to_all | solution.py:329
  74.2 6.2 %all-to-all-start.3 = ((bf16[32,8,4096]{2,1,0:T(8,128)(2,1)}), bf16[32,8,4096]{2,1,0:T(8,128)(2,1)}, u32[]{:S(2)}, u32[]{:S(2)}) async-start(bf16[32,8,4096]{2,1,0:T(8,128)(2,1)} %bitcast.29), calls=%async_computation.3 | async-start | bytes 4194304 | tf_op jit(solution)/shard_map/all_to_all | solution.py:329
  80.5 15.9 %feed_forward.2 = bf16[256,4096]{1,0:T(8,128)(2,1)} custom-call(s32[2]{0:T(128)} %copy-done.2, bf16[256,4096]{1,0:T(8,128)(2,1)} %bitcast.7.x_ref, bf16[4096,768]{1,0:T(8,128)(2,1)} %wg_ref.3, bf16[4096,768]{1,0:T(8,128)(2,1)} %wu_ref.3, bf16[768,4096]{1,0:T(8,128)(2,1)} %wd_ref.3, bf16[224,2304]{1,0:T(8,128)(2,1)} %copy-done, bf16[224,2304]{1,0:T(8,128)(2,1)} %copy-done.1), custom_call_target="tpu_custom_call" | custom-call | flops 4831838208 | bytes 29360128 | tf_op jit(solution)/shard_map/feed_forward/pallas_call | solution.py:206
  96.3 13.1 %all-to-all-done.3 = bf16[32,8,4096]{2,1,0:T(8,128)(2,1)} async-done(((bf16[32,8,4096]{2,1,0:T(8,128)(2,1)}), bf16[32,8,4096]{2,1,0:T(8,128)(2,1)}, u32[]{:S(2)}, u32[]{:S(2)}) %all-to-all-start.3) | async-done | bytes 2097184 | tf_op jit(solution)/shard_map/all_to_all | solution.py:329
  109.4 4.8 %all-to-all-start.2 = ((bf16[32,8,4096]{2,1,0:T(8,128)(2,1)}), bf16[32,8,4096]{2,1,0:T(8,128)(2,1)S(1)}, u32[]{:S(2)}, u32[]{:S(2)}) async-start(bf16[32,8,4096]{2,1,0:T(8,128)(2,1)} %bitcast.28), calls=%async_computation.2 | async-start | bytes 4194304 | tf_op jit(solution)/shard_map/all_to_all | solution.py:329
  114.2 1.7 %mixing.1 = bf16[2,64,256]{2,1,0:T(8,128)(2,1)} custom-call(s32[4,1024]{1,0:T(4,128)} %bitcast.34, f32[4,1024]{1,0:T(4,128)} %bitcast.39), custom_call_target="tpu_custom_call" | custom-call | flops 1048576 | bytes 131072 | tf_op jit(solution)/shard_map/mixing/pallas_call | solution.py:110
  115.9 0.8 slice_bitcast_fusion
  116.7 2.1 %combine.2.refs_0_ = f32[32,4096]{1,0:T(8,128)S(1)} custom-call(bf16[64,256]{1,0:T(8,128)(2,1)S(1)} %get-tuple-element.15.mix_ref, bf16[256,4096]{1,0:T(8,128)(2,1)} %bitcast.18.part_ref), custom_call_target="tpu_custom_call" | custom-call | flops 134217728 | bytes 3145728 | tf_op jit(solution)/shard_map/combine/pallas_call | solution.py:262
  118.7 24.4 %all-to-all-done.2 = bf16[32,8,4096]{2,1,0:T(8,128)(2,1)S(1)} async-done(((bf16[32,8,4096]{2,1,0:T(8,128)(2,1)}), bf16[32,8,4096]{2,1,0:T(8,128)(2,1)S(1)}, u32[]{:S(2)}, u32[]{:S(2)}) %all-to-all-start.2) | async-done | bytes 2097184 | tf_op jit(solution)/shard_map/all_to_all | solution.py:329
  143.1 1.2 combine.3
  (21 shorter events, 0.8 us)
Async XLA Ops:
  2.8 9.7 %copy-start.4 = (bf16[2,1024,32]{1,2,0:T(8,128)(2,1)S(1)}, bf16[2,1024,32]{1,2,0:T(8,128)(2,1)}, u32[]{:S(2)}) copy-start(bf16[2,1024,32]{1,2,0:T(8,128)(2,1)} %param.18) | copy-start | bytes 393220
  2.8 9.7 %copy-start.5 = (bf16[2,16,768]{2,1,0:T(8,128)(2,1)S(1)}, bf16[2,16,768]{2,1,0:T(8,128)(2,1)}, u32[]{:S(2)}) copy-start(bf16[2,16,768]{2,1,0:T(8,128)(2,1)} %param.19) | copy-start | bytes 147460
  2.8 9.7 %copy-start.3 = (bf16[16,2048]{1,0:T(8,128)(2,1)S(1)}, bf16[16,2048]{1,0:T(8,128)(2,1)}, u32[]{:S(2)}) copy-start(bf16[16,2048]{1,0:T(8,128)(2,1)} %param.21) | copy-start | bytes 196612
  2.8 9.7 %copy-start.6 = (bf16[768,16]{0,1:T(8,128)(2,1)S(1)}, bf16[768,16]{0,1:T(8,128)(2,1)}, u32[]{:S(2)}) copy-start(bf16[768,16]{0,1:T(8,128)(2,1)} %param.20) | copy-start | bytes 73732
  2.8 38.3 %all-to-all-start.1 = ((bf16[32,8,4096]{2,1,0:T(8,128)(2,1)}), bf16[32,8,4096]{2,1,0:T(8,128)(2,1)}, u32[]{:S(2)}, u32[]{:S(2)}) async-start(bf16[32,8,4096]{2,1,0:T(8,128)(2,1)} %bitcast.27), calls=%async_computation.1 | async-start | bytes 4194304 | tf_op jit(solution)/shard_map/all_to_all | solution.py:329
  13.3 37.8 %collective-permute-start = (bf16[64,2304]{1,0:T(8,128)(2,1)}, bf16[64,2304]{1,0:T(8,128)(2,1)}, u32[]{:S(2)}, u32[]{:S(2)}) collective-permute-start(bf16[64,2304]{1,0:T(8,128)(2,1)} %fusion.4), channel_id=1, source_target_pairs={{0,64},{32,96},{64,0},{96,32},{1,65},{33,97},{65,1},{97,33},{2,66}... | collective-permute-start | bytes 884744 | tf_op jit(solution)/shard_map/ppermute | solution.py:25
  16.7 34.4 %collective-permute-start.2 = (bf16[48,2048]{1,0:T(8,128)(2,1)}, bf16[48,2048]{1,0:T(8,128)(2,1)}, u32[]{:S(2)}, u32[]{:S(2)}) collective-permute-start(bf16[48,2048]{1,0:T(8,128)(2,1)} %constant_dynamic-update-slice_fusion), channel_id=1, source_target_pairs={{0,65},{1,64},{2,67},{3,66},{4,69},{5,68},{6,71},{7,70},{8,73},{9,... | collective-permute-start | bytes 589832 | tf_op jit(solution)/shard_map/ppermute | solution.py:300
  19.0 32.1 %collective-permute-start.1 = (bf16[48,2048]{1,0:T(8,128)(2,1)}, bf16[48,2048]{1,0:T(8,128)(2,1)}, u32[]{:S(2)}, u32[]{:S(2)}) collective-permute-start(bf16[48,2048]{1,0:T(8,128)(2,1)} %constant_dynamic-update-slice_fusion), channel_id=1, source_target_pairs={{0,1},{1,0},{2,3},{3,2},{4,5},{5,4},{6,7},{7,6},{8,9},{9,8},{10,11... | collective-permute-start | bytes 589832 | tf_op jit(solution)/shard_map/ppermute | solution.py:25
  41.1 33.2 %all-to-all-start = ((bf16[32,8,4096]{2,1,0:T(8,128)(2,1)}), bf16[32,8,4096]{2,1,0:T(8,128)(2,1)}, u32[]{:S(2)}, u32[]{:S(2)}) async-start(bf16[32,8,4096]{2,1,0:T(8,128)(2,1)} %bitcast.26), calls=%async_computation | async-start | bytes 4194304 | tf_op jit(solution)/shard_map/all_to_all | solution.py:329
  52.4 17.5 %copy-start = (bf16[224,2304]{1,0:T(8,128)(2,1)}, bf16[224,2304]{1,0:T(8,128)(2,1)S(1)}, u32[]{:S(2)}) copy-start(bf16[224,2304]{1,0:T(8,128)(2,1)S(1)} %pad_add_fusion.own_ref) | copy-start | bytes 3096580
  52.4 2.7 %collective-permute-start.3 = (bf16[224,2304]{1,0:T(8,128)(2,1)S(1)}, bf16[224,2304]{1,0:T(8,128)(2,1)S(1)}, u32[]{:S(2)}, u32[]{:S(2)}) collective-permute-start(bf16[224,2304]{1,0:T(8,128)(2,1)S(1)} %pad_add_fusion.own_ref), channel_id=1, source_target_pairs={{0,32},{32,0},{64,96},{96,64},{1,33},{33,1},{65,97},{97,65},{2,34}... | collective-permute-start | bytes 3096584 | tf_op jit(solution)/shard_map/ppermute | solution.py:25
  52.6 17.3 %copy-start.2 = (s32[2]{0:T(128)}, s32[2]{0:T(128)S(1)}, u32[]{:S(2)}) copy-start(s32[2]{0:T(128)S(1)} %pad_add_fusion.1.place_ref) | copy-start | bytes 28
  55.2 14.8 %copy-start.1 = (bf16[224,2304]{1,0:T(8,128)(2,1)}, bf16[224,2304]{1,0:T(8,128)(2,1)S(1)}, u32[]{:S(2)}) copy-start(bf16[224,2304]{1,0:T(8,128)(2,1)S(1)} %collective-permute-done.3.far_ref) | copy-start | bytes 3096580
  74.2 35.2 %all-to-all-start.3 = ((bf16[32,8,4096]{2,1,0:T(8,128)(2,1)}), bf16[32,8,4096]{2,1,0:T(8,128)(2,1)}, u32[]{:S(2)}, u32[]{:S(2)}) async-start(bf16[32,8,4096]{2,1,0:T(8,128)(2,1)} %bitcast.29), calls=%async_computation.3 | async-start | bytes 4194304 | tf_op jit(solution)/shard_map/all_to_all | solution.py:329
  109.4 33.7 %all-to-all-start.2 = ((bf16[32,8,4096]{2,1,0:T(8,128)(2,1)}), bf16[32,8,4096]{2,1,0:T(8,128)(2,1)S(1)}, u32[]{:S(2)}, u32[]{:S(2)}) async-start(bf16[32,8,4096]{2,1,0:T(8,128)(2,1)} %bitcast.28), calls=%async_computation.2 | async-start | bytes 4194304 | tf_op jit(solution)/shard_map/all_to_all | solution.py:329

commit v6 on v5

--- a/solution.py
+++ b/solution.py
@@ -63,9 +63,8 @@
     per = out_ref.shape[0]
     pick = mask_ref[pl.ds(pl.multiple_of(step * per * PART, per * PART), per * PART), :]
     rows = jnp.dot(pick, normed_ref[...], preferred_element_type=F32)
-    for i in range(per):
-        for half in range(2):
-            out_ref[i, half] = rows[i * PART : (i + 1) * PART].astype(BF16)
+    rows = rows.reshape(per, 1, PART, rows.shape[1]).astype(BF16)
+    out_ref[...] = jnp.broadcast_to(rows, out_ref.shape)
 
 
 def dispatch(tokens, gain, route_t, first):
@@ -199,7 +198,7 @@
 def feed_forward(place, x, wg, wu, wd, own, far, limit):
     rows, width = x.shape
     hidden = wg.shape[1]
-    span, cols = width // 4, 1024
+    span, cols = width // 4, 2048
     turn = lambda i, s: s[0] ^ jnp.minimum(i, 3)
     later = lambda i: jnp.maximum(i - 4, 0)
     whole = lambda a: pl.BlockSpec(a.shape, lambda i, s: (0,) * a.ndim)

time: 145 us -> 145 us (level)
  transfers between devices with their start and end apart: 8 -> 8, of which waited for: 6 -> 6; matrix products, arithmetic and copies ran while one was open for 3% -> 3% of each run, Pallas kernels for 26% -> 25%
where the time goes in v6:
time: 145 us; the launch traced here: 144 us
  waiting for transfers between devices  69.3 us (48%)
  Pallas kernels  39.8 us (27%)
  starting transfers between devices  30.7 us (21%)
  other arithmetic  2.16 us (1%)
  local copies, waits for them, and re-layouts  2.12 us (1%)
    all_to_all x4, waiting for transfers between devices, travel(): return lax.all_to_all(value, 'tensor', 0, 0, tiled=True).reshape(-1, width)  61.7 us
    pallas_call x2, Pallas kernels, feed_forward(): pl.pallas_call(ffn_body, grid_spec=pltpu.PrefetchScalarGridSpec(num_scala...  29.3 us
    all_to_all x4, starting transfers between devices, travel(): return lax.all_to_all(value, 'tensor', 0, 0, tiled=True).reshape(-1, width)  25.7 us
    pallas_call x2, Pallas kernels, dispatch(): pl.pallas_call(functools.partial(dispatch_body, first), grid=(steps,), ou...  5.6 us
    ppermute x1, waiting for transfers between devices, gather_factors(): corner = lax.ppermute(pair, ('group', 'tensor'), both)  5.06 us
    pallas_call x2, Pallas kernels, combine(): pl.pallas_call(combine_body, grid=(width // cols,), out_shape=jax.ShapeDt...  3.24 us
  transfers between devices with their start and end apart: 8, of which 6 were waited for; matrix products, arithmetic and copies ran while one was open for 3% of the time, Pallas kernels for 25%

profile of v6, /device:TPU:10, one launch (start us, length us, event | category | flops | bytes accessed | tf_op | source)
XLA Modules:
  0.0 144.3 jit_solution(2155157651326800311)
XLA Ops:
  0.0 2.8 %dispatch.3 = bf16[16,2,8,4096]{3,2,1,0:T(8,128)(2,1)} custom-call(bf16[32,4096]{1,0:T(8,128)(2,1)} %tokens_ref.3, f32[1,4096]{1,0:T(1,128)} %bitcast.36, s32[4,1024]{1,0:T(4,128)} %bitcast.32), custom_call_target="tpu_custom_call" | custom-call | flops 33554432 | bytes 3145728 | tf_op jit(solution)/shard_map/dispatch/pallas_call | solution.py:74
  2.8 9.7 %all-to-all-start.1 = ((bf16[32,8,4096]{2,1,0:T(8,128)(2,1)}), bf16[32,8,4096]{2,1,0:T(8,128)(2,1)}, u32[]{:S(2)}, u32[]{:S(2)}) async-start(bf16[32,8,4096]{2,1,0:T(8,128)(2,1)} %bitcast.27), calls=%async_computation.1 | async-start | bytes 4194304 | tf_op jit(solution)/shard_map/all_to_all | solution.py:328
  12.5 0.8 fusion.4
  13.3 2.1 %collective-permute-start = (bf16[64,2304]{1,0:T(8,128)(2,1)}, bf16[64,2304]{1,0:T(8,128)(2,1)}, u32[]{:S(2)}, u32[]{:S(2)}) collective-permute-start(bf16[64,2304]{1,0:T(8,128)(2,1)} %fusion.4), channel_id=1, source_target_pairs={{0,64},{32,96},{64,0},{96,32},{1,65},{33,97},{65,1},{97,33},{2,66}... | collective-permute-start | bytes 884744 | tf_op jit(solution)/shard_map/ppermute | solution.py:25
  15.4 0.7 constant_dynamic-update-slice_fusion.1
  16.1 0.6 constant_dynamic-update-slice_fusion
  16.7 2.3 %collective-permute-start.2 = (bf16[48,2048]{1,0:T(8,128)(2,1)}, bf16[48,2048]{1,0:T(8,128)(2,1)}, u32[]{:S(2)}, u32[]{:S(2)}) collective-permute-start(bf16[48,2048]{1,0:T(8,128)(2,1)} %constant_dynamic-update-slice_fusion), channel_id=1, source_target_pairs={{0,65},{1,64},{2,67},{3,66},{4,69},{5,68},{6,71},{7,70},{8,73},{9,... | collective-permute-start | bytes 589832 | tf_op jit(solution)/shard_map/ppermute | solution.py:299
  19.6 2.8 %dispatch.2 = bf16[16,2,8,4096]{3,2,1,0:T(8,128)(2,1)} custom-call(bf16[32,4096]{1,0:T(8,128)(2,1)} %tokens_ref.3, f32[1,4096]{1,0:T(1,128)} %bitcast.37, s32[4,1024]{1,0:T(4,128)} %bitcast.33), custom_call_target="tpu_custom_call" | custom-call | flops 33554432 | bytes 3145728 | tf_op jit(solution)/shard_map/dispatch/pallas_call | solution.py:74
  22.4 18.7 %all-to-all-done.1 = bf16[32,8,4096]{2,1,0:T(8,128)(2,1)} async-done(((bf16[32,8,4096]{2,1,0:T(8,128)(2,1)}), bf16[32,8,4096]{2,1,0:T(8,128)(2,1)}, u32[]{:S(2)}, u32[]{:S(2)}) %all-to-all-start.1) | async-done | bytes 2097184 | tf_op jit(solution)/shard_map/all_to_all | solution.py:328
  41.1 5.0 %all-to-all-start = ((bf16[32,8,4096]{2,1,0:T(8,128)(2,1)}), bf16[32,8,4096]{2,1,0:T(8,128)(2,1)}, u32[]{:S(2)}, u32[]{:S(2)}) async-start(bf16[32,8,4096]{2,1,0:T(8,128)(2,1)} %bitcast.26), calls=%async_computation | async-start | bytes 4194304 | tf_op jit(solution)/shard_map/all_to_all | solution.py:328
  46.1 5.1 %collective-permute-done.2 = bf16[48,2048]{1,0:T(8,128)(2,1)} collective-permute-done((bf16[48,2048]{1,0:T(8,128)(2,1)}, bf16[48,2048]{1,0:T(8,128)(2,1)}, u32[]{:S(2)}, u32[]{:S(2)}) %collective-permute-start.2) | collective-permute-done | bytes 196640 | tf_op jit(solution)/shard_map/ppermute | solution.py:299
  51.1 1.3 pad_add_fusion.own_ref
  52.6 2.5 %collective-permute-done.3.far_ref = bf16[224,2304]{1,0:T(8,128)(2,1)S(1)} collective-permute-done((bf16[224,2304]{1,0:T(8,128)(2,1)S(1)}, bf16[224,2304]{1,0:T(8,128)(2,1)S(1)}, u32[]{:S(2)}, u32[]{:S(2)}) %collective-permute-start.3) | collective-permute-done | bytes 1032224 | tf_op jit(solution)/shard_map/ppermute | solution.py:25
  55.2 14.1 %feed_forward.3 = bf16[256,4096]{1,0:T(8,128)(2,1)} custom-call(s32[2]{0:T(128)S(1)} %pad_add_fusion.1.place_ref, bf16[256,4096]{1,0:T(8,128)(2,1)} %bitcast.13.x_ref, bf16[4096,768]{1,0:T(8,128)(2,1)} %wg_ref.3, bf16[4096,768]{1,0:T(8,128)(2,1)} %wu_ref.3, bf16[768,4096]{1,0:T(8,128)(2,1)} %wd_ref.3, bf16[224,2304]{1,0:T(8,128)(2,1)S(1)} %pad_add_fusion.own_ref, ...), custom_call_target="tpu_custom_call" | custom-call | flops 4831838208 | bytes 29360128 | tf_op jit(solution)/shard_map/feed_forward/pallas_call | solution.py:205
  69.3 4.9 %all-to-all-done = bf16[32,8,4096]{2,1,0:T(8,128)(2,1)} async-done(((bf16[32,8,4096]{2,1,0:T(8,128)(2,1)}), bf16[32,8,4096]{2,1,0:T(8,128)(2,1)}, u32[]{:S(2)}, u32[]{:S(2)}) %all-to-all-start) | async-done | bytes 2097184 | tf_op jit(solution)/shard_map/all_to_all | solution.py:328
  74.2 6.2 %all-to-all-start.3 = ((bf16[32,8,4096]{2,1,0:T(8,128)(2,1)}), bf16[32,8,4096]{2,1,0:T(8,128)(2,1)}, u32[]{:S(2)}, u32[]{:S(2)}) async-start(bf16[32,8,4096]{2,1,0:T(8,128)(2,1)} %bitcast.29), calls=%async_computation.3 | async-start | bytes 4194304 | tf_op jit(solution)/shard_map/all_to_all | solution.py:328
  80.4 15.2 %feed_forward.2 = bf16[256,4096]{1,0:T(8,128)(2,1)} custom-call(s32[2]{0:T(128)} %copy-done.2, bf16[256,4096]{1,0:T(8,128)(2,1)} %bitcast.7.x_ref, bf16[4096,768]{1,0:T(8,128)(2,1)} %wg_ref.3, bf16[4096,768]{1,0:T(8,128)(2,1)} %wu_ref.3, bf16[768,4096]{1,0:T(8,128)(2,1)} %wd_ref.3, bf16[224,2304]{1,0:T(8,128)(2,1)} %copy-done, bf16[224,2304]{1,0:T(8,128)(2,1)} %copy-done.1), custom_call_target="tpu_custom_call" | custom-call | flops 4831838208 | bytes 29360128 | tf_op jit(solution)/shard_map/feed_forward/pallas_call | solution.py:205
  95.6 13.8 %all-to-all-done.3 = bf16[32,8,4096]{2,1,0:T(8,128)(2,1)} async-done(((bf16[32,8,4096]{2,1,0:T(8,128)(2,1)}), bf16[32,8,4096]{2,1,0:T(8,128)(2,1)}, u32[]{:S(2)}, u32[]{:S(2)}) %all-to-all-start.3) | async-done | bytes 2097184 | tf_op jit(solution)/shard_map/all_to_all | solution.py:328
  109.4 4.8 %all-to-all-start.2 = ((bf16[32,8,4096]{2,1,0:T(8,128)(2,1)}), bf16[32,8,4096]{2,1,0:T(8,128)(2,1)S(1)}, u32[]{:S(2)}, u32[]{:S(2)}) async-start(bf16[32,8,4096]{2,1,0:T(8,128)(2,1)} %bitcast.28), calls=%async_computation.2 | async-start | bytes 4194304 | tf_op jit(solution)/shard_map/all_to_all | solution.py:328
  114.2 1.7 %mixing.1 = bf16[2,64,256]{2,1,0:T(8,128)(2,1)} custom-call(s32[4,1024]{1,0:T(4,128)} %bitcast.34, f32[4,1024]{1,0:T(4,128)} %bitcast.39), custom_call_target="tpu_custom_call" | custom-call | flops 1048576 | bytes 131072 | tf_op jit(solution)/shard_map/mixing/pallas_call | solution.py:109
  115.9 0.8 slice_bitcast_fusion
  116.7 2.1 %combine.2.refs_0_ = f32[32,4096]{1,0:T(8,128)S(1)} custom-call(bf16[64,256]{1,0:T(8,128)(2,1)S(1)} %get-tuple-element.15.mix_ref, bf16[256,4096]{1,0:T(8,128)(2,1)} %bitcast.18.part_ref), custom_call_target="tpu_custom_call" | custom-call | flops 134217728 | bytes 3145728 | tf_op jit(solution)/shard_map/combine/pallas_call | solution.py:261
  118.7 24.4 %all-to-all-done.2 = bf16[32,8,4096]{2,1,0:T(8,128)(2,1)S(1)} async-done(((bf16[32,8,4096]{2,1,0:T(8,128)(2,1)}), bf16[32,8,4096]{2,1,0:T(8,128)(2,1)S(1)}, u32[]{:S(2)}, u32[]{:S(2)}) %all-to-all-start.2) | async-done | bytes 2097184 | tf_op jit(solution)/shard_map/all_to_all | solution.py:328
  143.1 1.2 combine.3
  (21 shorter events, 0.8 us)
Async XLA Ops:
  2.8 9.7 %copy-start.4 = (bf16[2,1024,32]{1,2,0:T(8,128)(2,1)S(1)}, bf16[2,1024,32]{1,2,0:T(8,128)(2,1)}, u32[]{:S(2)}) copy-start(bf16[2,1024,32]{1,2,0:T(8,128)(2,1)} %param.18) | copy-start | bytes 393220
  2.8 9.7 %copy-start.5 = (bf16[2,16,768]{2,1,0:T(8,128)(2,1)S(1)}, bf16[2,16,768]{2,1,0:T(8,128)(2,1)}, u32[]{:S(2)}) copy-start(bf16[2,16,768]{2,1,0:T(8,128)(2,1)} %param.19) | copy-start | bytes 147460
  2.8 9.7 %copy-start.3 = (bf16[16,2048]{1,0:T(8,128)(2,1)S(1)}, bf16[16,2048]{1,0:T(8,128)(2,1)}, u32[]{:S(2)}) copy-start(bf16[16,2048]{1,0:T(8,128)(2,1)} %param.21) | copy-start | bytes 196612
  2.8 9.7 %copy-start.6 = (bf16[768,16]{0,1:T(8,128)(2,1)S(1)}, bf16[768,16]{0,1:T(8,128)(2,1)}, u32[]{:S(2)}) copy-start(bf16[768,16]{0,1:T(8,128)(2,1)} %param.20) | copy-start | bytes 73732
  2.8 38.3 %all-to-all-start.1 = ((bf16[32,8,4096]{2,1,0:T(8,128)(2,1)}), bf16[32,8,4096]{2,1,0:T(8,128)(2,1)}, u32[]{:S(2)}, u32[]{:S(2)}) async-start(bf16[32,8,4096]{2,1,0:T(8,128)(2,1)} %bitcast.27), calls=%async_computation.1 | async-start | bytes 4194304 | tf_op jit(solution)/shard_map/all_to_all | solution.py:328
  13.3 37.8 %collective-permute-start = (bf16[64,2304]{1,0:T(8,128)(2,1)}, bf16[64,2304]{1,0:T(8,128)(2,1)}, u32[]{:S(2)}, u32[]{:S(2)}) collective-permute-start(bf16[64,2304]{1,0:T(8,128)(2,1)} %fusion.4), channel_id=1, source_target_pairs={{0,64},{32,96},{64,0},{96,32},{1,65},{33,97},{65,1},{97,33},{2,66}... | collective-permute-start | bytes 884744 | tf_op jit(solution)/shard_map/ppermute | solution.py:25
  16.7 34.4 %collective-permute-start.2 = (bf16[48,2048]{1,0:T(8,128)(2,1)}, bf16[48,2048]{1,0:T(8,128)(2,1)}, u32[]{:S(2)}, u32[]{:S(2)}) collective-permute-start(bf16[48,2048]{1,0:T(8,128)(2,1)} %constant_dynamic-update-slice_fusion), channel_id=1, source_target_pairs={{0,65},{1,64},{2,67},{3,66},{4,69},{5,68},{6,71},{7,70},{8,73},{9,... | collective-permute-start | bytes 589832 | tf_op jit(solution)/shard_map/ppermute | solution.py:299
  19.0 32.1 %collective-permute-start.1 = (bf16[48,2048]{1,0:T(8,128)(2,1)}, bf16[48,2048]{1,0:T(8,128)(2,1)}, u32[]{:S(2)}, u32[]{:S(2)}) collective-permute-start(bf16[48,2048]{1,0:T(8,128)(2,1)} %constant_dynamic-update-slice_fusion), channel_id=1, source_target_pairs={{0,1},{1,0},{2,3},{3,2},{4,5},{5,4},{6,7},{7,6},{8,9},{9,8},{10,11... | collective-permute-start | bytes 589832 | tf_op jit(solution)/shard_map/ppermute | solution.py:25
  41.1 33.1 %all-to-all-start = ((bf16[32,8,4096]{2,1,0:T(8,128)(2,1)}), bf16[32,8,4096]{2,1,0:T(8,128)(2,1)}, u32[]{:S(2)}, u32[]{:S(2)}) async-start(bf16[32,8,4096]{2,1,0:T(8,128)(2,1)} %bitcast.26), calls=%async_computation | async-start | bytes 4194304 | tf_op jit(solution)/shard_map/all_to_all | solution.py:328
  52.5 16.8 %copy-start = (bf16[224,2304]{1,0:T(8,128)(2,1)}, bf16[224,2304]{1,0:T(8,128)(2,1)S(1)}, u32[]{:S(2)}) copy-start(bf16[224,2304]{1,0:T(8,128)(2,1)S(1)} %pad_add_fusion.own_ref) | copy-start | bytes 3096580
  52.5 2.7 %collective-permute-start.3 = (bf16[224,2304]{1,0:T(8,128)(2,1)S(1)}, bf16[224,2304]{1,0:T(8,128)(2,1)S(1)}, u32[]{:S(2)}, u32[]{:S(2)}) collective-permute-start(bf16[224,2304]{1,0:T(8,128)(2,1)S(1)} %pad_add_fusion.own_ref), channel_id=1, source_target_pairs={{0,32},{32,0},{64,96},{96,64},{1,33},{33,1},{65,97},{97,65},{2,34}... | collective-permute-start | bytes 3096584 | tf_op jit(solution)/shard_map/ppermute | solution.py:25
  52.6 16.7 %copy-start.2 = (s32[2]{0:T(128)}, s32[2]{0:T(128)S(1)}, u32[]{:S(2)}) copy-start(s32[2]{0:T(128)S(1)} %pad_add_fusion.1.place_ref) | copy-start | bytes 28
  55.2 14.1 %copy-start.1 = (bf16[224,2304]{1,0:T(8,128)(2,1)}, bf16[224,2304]{1,0:T(8,128)(2,1)S(1)}, u32[]{:S(2)}) copy-start(bf16[224,2304]{1,0:T(8,128)(2,1)S(1)} %collective-permute-done.3.far_ref) | copy-start | bytes 3096580
  74.2 35.2 %all-to-all-start.3 = ((bf16[32,8,4096]{2,1,0:T(8,128)(2,1)}), bf16[32,8,4096]{2,1,0:T(8,128)(2,1)}, u32[]{:S(2)}, u32[]{:S(2)}) async-start(bf16[32,8,4096]{2,1,0:T(8,128)(2,1)} %bitcast.29), calls=%async_computation.3 | async-start | bytes 4194304 | tf_op jit(solution)/shard_map/all_to_all | solution.py:328
  109.4 33.7 %all-to-all-start.2 = ((bf16[32,8,4096]{2,1,0:T(8,128)(2,1)}), bf16[32,8,4096]{2,1,0:T(8,128)(2,1)S(1)}, u32[]{:S(2)}, u32[]{:S(2)}) async-start(bf16[32,8,4096]{2,1,0:T(8,128)(2,1)} %bitcast.28), calls=%async_computation.2 | async-start | bytes 4194304 | tf_op jit(solution)/shard_map/all_to_all | solution.py:328

commit v7 on v6

--- a/solution.py
+++ b/solution.py
@@ -245,13 +245,13 @@
     out_ref[...] = total.astype(out_ref.dtype)
 
 
-def combine(mix, part, base, out_type):
+def combine(mix, which, part, base, out_type):
     slots, width = part.shape
-    rows = mix.shape[0] // 2
+    rows = mix.shape[1] // 2
     cols = width
     sheet = pl.BlockSpec((rows, cols), lambda i: (0, i))
     in_specs = [
-        pl.BlockSpec(mix.shape, lambda i: (0, 0)),
+        pl.BlockSpec((None, *mix.shape[1:]), lambda i: (which, 0, 0)),
         pl.BlockSpec((slots, cols), lambda i: (0, i)),
     ]
     operands = (mix, part)
@@ -336,8 +336,8 @@
         travel(feed_forward(place, x, *weights, own, far, limit))
         for x, limit in zip(arrived, FFN_VMEM)
     ]
-    base = combine(mix[0], parts[0], None, F32)
-    return combine(mix[1], parts[1], base, BF16)
+    base = combine(mix, 0, parts[0], None, F32)
+    return combine(mix, 1, parts[1], base, BF16)
 
 
 def solution(mesh):

time: 145 us -> 145 us (level)
  transfers between devices with their start and end apart: 8 -> 8, of which waited for: 6 -> 6; matrix products, arithmetic and copies ran while one was open for 3% -> 2% of each run, Pallas kernels for 25% -> 25%
where the time goes in v7:
time: 145 us; the launch traced here: 144 us
  waiting for transfers between devices  69.4 us (48%)
  Pallas kernels  39.7 us (27%)
  starting transfers between devices  30.7 us (21%)
  local copies, waits for them, and re-layouts  2.18 us (2%)
  other arithmetic  2.14 us (1%)
    all_to_all x4, waiting for transfers between devices, travel(): return lax.all_to_all(value, 'tensor', 0, 0, tiled=True).reshape(-1, width)  61.8 us
    pallas_call x2, Pallas kernels, feed_forward(): pl.pallas_call(ffn_body, grid_spec=pltpu.PrefetchScalarGridSpec(num_scala...  29.2 us
    all_to_all x4, starting transfers between devices, travel(): return lax.all_to_all(value, 'tensor', 0, 0, tiled=True).reshape(-1, width)  25.7 us
    pallas_call x2, Pallas kernels, dispatch(): pl.pallas_call(functools.partial(dispatch_body, first), grid=(steps,), ou...  5.59 us
    ppermute x1, waiting for transfers between devices, gather_factors(): corner = lax.ppermute(pair, ('group', 'tensor'), both)  5.06 us
    pallas_call x2, Pallas kernels, combine(): pl.pallas_call(combine_body, grid=(width // cols,), out_shape=jax.ShapeDt...  3.27 us
  transfers between devices with their start and end apart: 8, of which 6 were waited for; matrix products, arithmetic and copies ran while one was open for 2% of the time, Pallas kernels for 25%

profile of v7, /device:TPU:10, one launch (start us, length us, event | category | flops | bytes accessed | tf_op | source)
XLA Modules:
  0.0 144.3 jit_solution(14819090043646546714)
XLA Ops:
  0.0 2.8 %dispatch.3 = bf16[16,2,8,4096]{3,2,1,0:T(8,128)(2,1)} custom-call(bf16[32,4096]{1,0:T(8,128)(2,1)} %tokens_ref.3, f32[1,4096]{1,0:T(1,128)} %bitcast.32, s32[4,1024]{1,0:T(4,128)} %bitcast.28), custom_call_target="tpu_custom_call" | custom-call | flops 33554432 | bytes 3145728 | tf_op jit(solution)/shard_map/dispatch/pallas_call | solution.py:74
  2.8 9.7 %all-to-all-start.1 = ((bf16[32,8,4096]{2,1,0:T(8,128)(2,1)}), bf16[32,8,4096]{2,1,0:T(8,128)(2,1)}, u32[]{:S(2)}, u32[]{:S(2)}) async-start(bf16[32,8,4096]{2,1,0:T(8,128)(2,1)} %bitcast.23), calls=%async_computation.1 | async-start | bytes 4194304 | tf_op jit(solution)/shard_map/all_to_all | solution.py:328
  12.5 0.7 fusion.4
  13.3 2.1 %collective-permute-start = (bf16[64,2304]{1,0:T(8,128)(2,1)}, bf16[64,2304]{1,0:T(8,128)(2,1)}, u32[]{:S(2)}, u32[]{:S(2)}) collective-permute-start(bf16[64,2304]{1,0:T(8,128)(2,1)} %fusion.4), channel_id=1, source_target_pairs={{0,64},{32,96},{64,0},{96,32},{1,65},{33,97},{65,1},{97,33},{2,66}... | collective-permute-start | bytes 884744 | tf_op jit(solution)/shard_map/ppermute | solution.py:25
  15.4 0.7 constant_dynamic-update-slice_fusion.1
  16.1 0.6 constant_dynamic-update-slice_fusion
  16.7 2.3 %collective-permute-start.2 = (bf16[48,2048]{1,0:T(8,128)(2,1)}, bf16[48,2048]{1,0:T(8,128)(2,1)}, u32[]{:S(2)}, u32[]{:S(2)}) collective-permute-start(bf16[48,2048]{1,0:T(8,128)(2,1)} %constant_dynamic-update-slice_fusion), channel_id=1, source_target_pairs={{0,65},{1,64},{2,67},{3,66},{4,69},{5,68},{6,71},{7,70},{8,73},{9,... | collective-permute-start | bytes 589832 | tf_op jit(solution)/shard_map/ppermute | solution.py:299
  19.6 2.8 %dispatch.2 = bf16[16,2,8,4096]{3,2,1,0:T(8,128)(2,1)} custom-call(bf16[32,4096]{1,0:T(8,128)(2,1)} %tokens_ref.3, f32[1,4096]{1,0:T(1,128)} %bitcast.33, s32[4,1024]{1,0:T(4,128)} %bitcast.29), custom_call_target="tpu_custom_call" | custom-call | flops 33554432 | bytes 3145728 | tf_op jit(solution)/shard_map/dispatch/pallas_call | solution.py:74
  22.4 18.7 %all-to-all-done.1 = bf16[32,8,4096]{2,1,0:T(8,128)(2,1)} async-done(((bf16[32,8,4096]{2,1,0:T(8,128)(2,1)}), bf16[32,8,4096]{2,1,0:T(8,128)(2,1)}, u32[]{:S(2)}, u32[]{:S(2)}) %all-to-all-start.1) | async-done | bytes 2097184 | tf_op jit(solution)/shard_map/all_to_all | solution.py:328
  41.1 5.0 %all-to-all-start = ((bf16[32,8,4096]{2,1,0:T(8,128)(2,1)}), bf16[32,8,4096]{2,1,0:T(8,128)(2,1)}, u32[]{:S(2)}, u32[]{:S(2)}) async-start(bf16[32,8,4096]{2,1,0:T(8,128)(2,1)} %bitcast.22), calls=%async_computation | async-start | bytes 4194304 | tf_op jit(solution)/shard_map/all_to_all | solution.py:328
  46.1 5.1 %collective-permute-done.2 = bf16[48,2048]{1,0:T(8,128)(2,1)} collective-permute-done((bf16[48,2048]{1,0:T(8,128)(2,1)}, bf16[48,2048]{1,0:T(8,128)(2,1)}, u32[]{:S(2)}, u32[]{:S(2)}) %collective-permute-start.2) | collective-permute-done | bytes 196640 | tf_op jit(solution)/shard_map/ppermute | solution.py:299
  51.1 1.3 pad_add_fusion.own_ref
  52.6 2.5 %collective-permute-done.3.far_ref = bf16[224,2304]{1,0:T(8,128)(2,1)S(1)} collective-permute-done((bf16[224,2304]{1,0:T(8,128)(2,1)S(1)}, bf16[224,2304]{1,0:T(8,128)(2,1)S(1)}, u32[]{:S(2)}, u32[]{:S(2)}) %collective-permute-start.3) | collective-permute-done | bytes 1032224 | tf_op jit(solution)/shard_map/ppermute | solution.py:25
  55.2 14.1 %feed_forward.3 = bf16[256,4096]{1,0:T(8,128)(2,1)} custom-call(s32[2]{0:T(128)S(1)} %pad_add_fusion.1.place_ref, bf16[256,4096]{1,0:T(8,128)(2,1)} %bitcast.12.x_ref, bf16[4096,768]{1,0:T(8,128)(2,1)} %wg_ref.3, bf16[4096,768]{1,0:T(8,128)(2,1)} %wu_ref.3, bf16[768,4096]{1,0:T(8,128)(2,1)} %wd_ref.3, bf16[224,2304]{1,0:T(8,128)(2,1)S(1)} %pad_add_fusion.own_ref, ...), custom_call_target="tpu_custom_call" | custom-call | flops 4831838208 | bytes 29360128 | tf_op jit(solution)/shard_map/feed_forward/pallas_call | solution.py:205
  69.3 5.0 %all-to-all-done = bf16[32,8,4096]{2,1,0:T(8,128)(2,1)} async-done(((bf16[32,8,4096]{2,1,0:T(8,128)(2,1)}), bf16[32,8,4096]{2,1,0:T(8,128)(2,1)}, u32[]{:S(2)}, u32[]{:S(2)}) %all-to-all-start) | async-done | bytes 2097184 | tf_op jit(solution)/shard_map/all_to_all | solution.py:328
  74.2 6.2 %all-to-all-start.3 = ((bf16[32,8,4096]{2,1,0:T(8,128)(2,1)}), bf16[32,8,4096]{2,1,0:T(8,128)(2,1)}, u32[]{:S(2)}, u32[]{:S(2)}) async-start(bf16[32,8,4096]{2,1,0:T(8,128)(2,1)} %bitcast.25), calls=%async_computation.3 | async-start | bytes 4194304 | tf_op jit(solution)/shard_map/all_to_all | solution.py:328
  80.4 15.1 %feed_forward.2 = bf16[256,4096]{1,0:T(8,128)(2,1)} custom-call(s32[2]{0:T(128)} %copy-done.4, bf16[256,4096]{1,0:T(8,128)(2,1)} %bitcast.6.x_ref, bf16[4096,768]{1,0:T(8,128)(2,1)} %wg_ref.3, bf16[4096,768]{1,0:T(8,128)(2,1)} %wu_ref.3, bf16[768,4096]{1,0:T(8,128)(2,1)} %wd_ref.3, bf16[224,2304]{1,0:T(8,128)(2,1)} %copy-done, bf16[224,2304]{1,0:T(8,128)(2,1)} %copy-done.1), custom_call_target="tpu_custom_call" | custom-call | flops 4831838208 | bytes 29360128 | tf_op jit(solution)/shard_map/feed_forward/pallas_call | solution.py:205
  95.5 13.8 %all-to-all-done.3 = bf16[32,8,4096]{2,1,0:T(8,128)(2,1)} async-done(((bf16[32,8,4096]{2,1,0:T(8,128)(2,1)}), bf16[32,8,4096]{2,1,0:T(8,128)(2,1)}, u32[]{:S(2)}, u32[]{:S(2)}) %all-to-all-start.3) | async-done | bytes 2097184 | tf_op jit(solution)/shard_map/all_to_all | solution.py:328
  109.4 4.8 %all-to-all-start.2 = ((bf16[32,8,4096]{2,1,0:T(8,128)(2,1)}), bf16[32,8,4096]{2,1,0:T(8,128)(2,1)S(1)}, u32[]{:S(2)}, u32[]{:S(2)}) async-start(bf16[32,8,4096]{2,1,0:T(8,128)(2,1)} %bitcast.24), calls=%async_computation.2 | async-start | bytes 4194304 | tf_op jit(solution)/shard_map/all_to_all | solution.py:328
  114.2 1.7 %mixing.1.mix_ref = bf16[2,64,256]{2,1,0:T(8,128)(2,1)} custom-call(s32[4,1024]{1,0:T(4,128)} %bitcast.30, f32[4,1024]{1,0:T(4,128)} %bitcast.35), custom_call_target="tpu_custom_call" | custom-call | flops 1048576 | bytes 131072 | tf_op jit(solution)/shard_map/mixing/pallas_call | solution.py:109
  115.9 0.8 copy-done.2
  116.7 2.1 %combine.2.refs_0_ = f32[32,4096]{1,0:T(8,128)S(1)} custom-call(bf16[2,64,256]{2,1,0:T(8,128)(2,1)S(1)} %copy-done.2, bf16[256,4096]{1,0:T(8,128)(2,1)} %bitcast.16.part_ref), custom_call_target="tpu_custom_call" | custom-call | flops 134217728 | bytes 3145728 | tf_op jit(solution)/shard_map/combine/pallas_call | solution.py:261
  118.8 24.3 %all-to-all-done.2 = bf16[32,8,4096]{2,1,0:T(8,128)(2,1)S(1)} async-done(((bf16[32,8,4096]{2,1,0:T(8,128)(2,1)}), bf16[32,8,4096]{2,1,0:T(8,128)(2,1)S(1)}, u32[]{:S(2)}, u32[]{:S(2)}) %all-to-all-start.2) | async-done | bytes 2097184 | tf_op jit(solution)/shard_map/all_to_all | solution.py:328
  143.1 1.2 combine.3
  (24 shorter events, 0.8 us)
Async XLA Ops:
  2.8 9.7 %copy-start.6 = (bf16[2,1024,32]{1,2,0:T(8,128)(2,1)S(1)}, bf16[2,1024,32]{1,2,0:T(8,128)(2,1)}, u32[]{:S(2)}) copy-start(bf16[2,1024,32]{1,2,0:T(8,128)(2,1)} %param.18) | copy-start | bytes 393220
  2.8 9.7 %copy-start.7 = (bf16[2,16,768]{2,1,0:T(8,128)(2,1)S(1)}, bf16[2,16,768]{2,1,0:T(8,128)(2,1)}, u32[]{:S(2)}) copy-start(bf16[2,16,768]{2,1,0:T(8,128)(2,1)} %param.19) | copy-start | bytes 147460
  2.8 9.7 %copy-start.5 = (bf16[16,2048]{1,0:T(8,128)(2,1)S(1)}, bf16[16,2048]{1,0:T(8,128)(2,1)}, u32[]{:S(2)}) copy-start(bf16[16,2048]{1,0:T(8,128)(2,1)} %param.21) | copy-start | bytes 196612
  2.8 9.7 %copy-start.8 = (bf16[768,16]{0,1:T(8,128)(2,1)S(1)}, bf16[768,16]{0,1:T(8,128)(2,1)}, u32[]{:S(2)}) copy-start(bf16[768,16]{0,1:T(8,128)(2,1)} %param.20) | copy-start | bytes 73732
  2.8 38.3 %all-to-all-start.1 = ((bf16[32,8,4096]{2,1,0:T(8,128)(2,1)}), bf16[32,8,4096]{2,1,0:T(8,128)(2,1)}, u32[]{:S(2)}, u32[]{:S(2)}) async-start(bf16[32,8,4096]{2,1,0:T(8,128)(2,1)} %bitcast.23), calls=%async_computation.1 | async-start | bytes 4194304 | tf_op jit(solution)/shard_map/all_to_all | solution.py:328
  13.3 37.8 %collective-permute-start = (bf16[64,2304]{1,0:T(8,128)(2,1)}, bf16[64,2304]{1,0:T(8,128)(2,1)}, u32[]{:S(2)}, u32[]{:S(2)}) collective-permute-start(bf16[64,2304]{1,0:T(8,128)(2,1)} %fusion.4), channel_id=1, source_target_pairs={{0,64},{32,96},{64,0},{96,32},{1,65},{33,97},{65,1},{97,33},{2,66}... | collective-permute-start | bytes 884744 | tf_op jit(solution)/shard_map/ppermute | solution.py:25
  16.7 34.4 %collective-permute-start.2 = (bf16[48,2048]{1,0:T(8,128)(2,1)}, bf16[48,2048]{1,0:T(8,128)(2,1)}, u32[]{:S(2)}, u32[]{:S(2)}) collective-permute-start(bf16[48,2048]{1,0:T(8,128)(2,1)} %constant_dynamic-update-slice_fusion), channel_id=1, source_target_pairs={{0,65},{1,64},{2,67},{3,66},{4,69},{5,68},{6,71},{7,70},{8,73},{9,... | collective-permute-start | bytes 589832 | tf_op jit(solution)/shard_map/ppermute | solution.py:299
  19.0 32.1 %collective-permute-start.1 = (bf16[48,2048]{1,0:T(8,128)(2,1)}, bf16[48,2048]{1,0:T(8,128)(2,1)}, u32[]{:S(2)}, u32[]{:S(2)}) collective-permute-start(bf16[48,2048]{1,0:T(8,128)(2,1)} %constant_dynamic-update-slice_fusion), channel_id=1, source_target_pairs={{0,1},{1,0},{2,3},{3,2},{4,5},{5,4},{6,7},{7,6},{8,9},{9,8},{10,11... | collective-permute-start | bytes 589832 | tf_op jit(solution)/shard_map/ppermute | solution.py:25
  41.1 33.1 %all-to-all-start = ((bf16[32,8,4096]{2,1,0:T(8,128)(2,1)}), bf16[32,8,4096]{2,1,0:T(8,128)(2,1)}, u32[]{:S(2)}, u32[]{:S(2)}) async-start(bf16[32,8,4096]{2,1,0:T(8,128)(2,1)} %bitcast.22), calls=%async_computation | async-start | bytes 4194304 | tf_op jit(solution)/shard_map/all_to_all | solution.py:328
  52.4 16.8 %copy-start = (bf16[224,2304]{1,0:T(8,128)(2,1)}, bf16[224,2304]{1,0:T(8,128)(2,1)S(1)}, u32[]{:S(2)}) copy-start(bf16[224,2304]{1,0:T(8,128)(2,1)S(1)} %pad_add_fusion.own_ref) | copy-start | bytes 3096580
  52.5 2.7 %collective-permute-start.3 = (bf16[224,2304]{1,0:T(8,128)(2,1)S(1)}, bf16[224,2304]{1,0:T(8,128)(2,1)S(1)}, u32[]{:S(2)}, u32[]{:S(2)}) collective-permute-start(bf16[224,2304]{1,0:T(8,128)(2,1)S(1)} %pad_add_fusion.own_ref), channel_id=1, source_target_pairs={{0,32},{32,0},{64,96},{96,64},{1,33},{33,1},{65,97},{97,65},{2,34}... | collective-permute-start | bytes 3096584 | tf_op jit(solution)/shard_map/ppermute | solution.py:25
  52.6 16.6 %copy-start.4 = (s32[2]{0:T(128)}, s32[2]{0:T(128)S(1)}, u32[]{:S(2)}) copy-start(s32[2]{0:T(128)S(1)} %pad_add_fusion.1.place_ref) | copy-start | bytes 28
  55.2 14.1 %copy-start.1 = (bf16[224,2304]{1,0:T(8,128)(2,1)}, bf16[224,2304]{1,0:T(8,128)(2,1)S(1)}, u32[]{:S(2)}) copy-start(bf16[224,2304]{1,0:T(8,128)(2,1)S(1)} %collective-permute-done.3.far_ref) | copy-start | bytes 3096580
  74.2 35.2 %all-to-all-start.3 = ((bf16[32,8,4096]{2,1,0:T(8,128)(2,1)}), bf16[32,8,4096]{2,1,0:T(8,128)(2,1)}, u32[]{:S(2)}, u32[]{:S(2)}) async-start(bf16[32,8,4096]{2,1,0:T(8,128)(2,1)} %bitcast.25), calls=%async_computation.3 | async-start | bytes 4194304 | tf_op jit(solution)/shard_map/all_to_all | solution.py:328
  109.4 33.7 %all-to-all-start.2 = ((bf16[32,8,4096]{2,1,0:T(8,128)(2,1)}), bf16[32,8,4096]{2,1,0:T(8,128)(2,1)S(1)}, u32[]{:S(2)}, u32[]{:S(2)}) async-start(bf16[32,8,4096]{2,1,0:T(8,128)(2,1)} %bitcast.24), calls=%async_computation.2 | async-start | bytes 4194304 | tf_op jit(solution)/shard_map/all_to_all | solution.py:328
  115.9 0.8 copy-start.2
  116.7 26.4 %copy-start.3 = (bf16[2,64,256]{2,1,0:T(8,128)(2,1)S(1)}, bf16[2,64,256]{2,1,0:T(8,128)(2,1)}, u32[]{:S(2)}) copy-start(bf16[2,64,256]{2,1,0:T(8,128)(2,1)} %mixing.1.mix_ref) | copy-start | bytes 196612
